TPU v7x, 512 devices: a whole 4x4x16 slice. The times are simulated.
512 devices in a mesh: seq: 32 (over x, z_hi, core), tile: 16 (over y, z_lo).
Axes of the slice: x: 4, y: 4, z: 16 (z_hi: 4, z_lo: 4; z = z_hi * 4 + z_lo), core: 2. Of those that a mesh axis runs over, the one named last changes fastest.
Arguments:
- queries: bfloat16 [65536, 2048], P(('seq', 'tile')), may hold values from -192 to 192
- head_keys: bfloat16 [65536, 2048], P(('seq', 'tile')), may hold values from -6 to 6
- head_values: bfloat16 [65536, 2048], P(('seq', 'tile')), may hold values from -12 to 12
- region_request: int32 [65536], P(('seq', 'tile')), may hold values from 0 to 7
- request_adapter: int32 [8], replicated, may hold values from 0 to 3
- residual: bfloat16 [65536, 3072], P(('seq', 'tile')), may hold values from -3 to 3
- output_gate: float32 [3072], replicated, may hold values from 0.1 to 1.9
- output_weight: bfloat16 [2048, 3072], P(None, 'tile'), may hold values from -1.5 to 1.5
- adapter_down_factors: bfloat16 [2048, 128], replicated, may hold values from -0.125 to 0.125
- adapter_up_factors: bfloat16 [128, 3072], P(None, 'tile'), may hold values from -1.5 to 1.5
- closing_scale: float32 [3072], replicated, may hold values from -2.5 to 2.5
- closing_shift: float32 [3072], replicated, may hold values from -2.5 to 2.5
- patch_projection_weight: bfloat16 [3072, 64], replicated, may hold values from -0.0546875 to 0.0546875
- patch_projection_bias: float32 [64], replicated, may hold values from -2.5 to 2.5
- convolution_kernel: bfloat16 [3, 3, 16, 512], replicated, may hold values from -0.5 to 0.5
- convolution_bias: float32 [512], replicated, may hold values from -2.5 to 2.5
Outputs:
- decoded: bfloat16 [512, 512, 512], P('seq', 'tile')
All inputs are finite; a program needn't handle non-finite values.
Results may differ from a plain program's by a relative error of at most 0.015.
Values may be sent and summed in bfloat16 or wider, within the bound.
A program may use at most 64 MiB of HBM per device.

v0:
```python
import math

import jax
import jax.numpy as jnp
from jax import lax
from jax.sharding import PartitionSpec as P

HD = 128
LAT_CH = 16
ADAPTER_RANK = 32
LAT_W = 256
WIN = 512


norm_epsilon = 1e-06
latent_scaling = 0.3611
latent_offset = 0.1159


def with_halo(block, sides, width):
    for axis, dim in sides:
        count = lax.axis_size(axis)
        forward = [(i, i + 1) for i in range(count - 1)]
        backward = [(target, source) for source, target in forward]
        low = lax.ppermute(
            lax.slice_in_dim(block, block.shape[dim] - width, None, axis=dim), axis, forward
        )
        high = lax.ppermute(lax.slice_in_dim(block, 0, width, axis=dim), axis, backward)
        block = jnp.concatenate([low, block, high], axis=dim)
    return block


def band_attention(queries, key_rows, value_rows, first_token, token_total, window, head_size):
    row_count = queries.shape[0]
    block_rows = min(512, row_count)
    scaling = 1.0 / math.sqrt(head_size)

    def one_block(block_index):
        first_row = block_index * block_rows
        query_block = lax.dynamic_slice_in_dim(queries, first_row, block_rows, 0)
        key_block = lax.dynamic_slice_in_dim(key_rows, first_row, block_rows + 2 * window, 0)
        value_block = lax.dynamic_slice_in_dim(value_rows, first_row, block_rows + 2 * window, 0)
        scores = (
            jnp.einsum("qhd,khd->hqk", query_block, key_block, preferred_element_type=jnp.float32)
            * scaling
        )
        query_place = first_token + first_row + jnp.arange(block_rows, dtype=jnp.int32)
        key_place = (
            first_token - window + first_row + jnp.arange(block_rows + 2 * window, dtype=jnp.int32)
        )
        distance = jnp.abs(query_place[:, None] - key_place[None, :])
        allowed = (
            (distance <= window) & (key_place[None, :] >= 0) & (key_place[None, :] < token_total)
        )
        scores = jnp.where(allowed[None], scores, -jnp.inf)
        highest = jnp.max(scores, axis=2, keepdims=True)
        expons = jnp.exp(scores - highest)
        totals = jnp.sum(expons, axis=2)
        weights = expons.astype(jnp.bfloat16)
        weighted = jnp.einsum(
            "hqk,khd->qhd", weights, value_block, preferred_element_type=jnp.float32
        )
        return (weighted / jnp.transpose(totals)[:, :, None]).astype(jnp.bfloat16)

    pieces = lax.map(one_block, jnp.arange(row_count // block_rows, dtype=jnp.int32))
    return pieces.reshape(row_count, -1)


def adapter_of(region_request, request_adapter):
    request_cols = jnp.arange(request_adapter.shape[0], dtype=jnp.int32)
    matches = region_request[:, None] == request_cols[None, :]
    return jnp.sum(jnp.where(matches, request_adapter[None, :], 0), axis=1)


def mask_lowered(lowered_result, adapter_list, rank_width):
    owner_requests = jnp.arange(lowered_result.shape[1], dtype=jnp.int32) // rank_width
    kept_cols = adapter_list[:, None] == owner_requests[None, :]
    return jnp.where(kept_cols, lowered_result, 0.0).astype(jnp.bfloat16)


def reduced_rank(attended_heads, adapter_down_factors, adapter_list, rank_width):
    lowered_result = jnp.dot(
        attended_heads, adapter_down_factors, preferred_element_type=jnp.float32
    )
    return mask_lowered(lowered_result, adapter_list, rank_width)


def patch_latents(
    block_out, closing_scale, closing_shift, patch_projection_weight, patch_projection_bias
):
    block_values = block_out.astype(jnp.float32)
    average = jnp.mean(block_values, axis=1, keepdims=True)
    centered = block_values - average
    variance = jnp.mean(centered * centered, axis=1, keepdims=True)
    modulated = (
        centered * lax.rsqrt(variance + norm_epsilon) * (1.0 + closing_scale) + closing_shift
    ).astype(jnp.bfloat16)
    projected = (
        jnp.dot(modulated, patch_projection_weight, preferred_element_type=jnp.float32)
        + patch_projection_bias
    )
    return (projected / latent_scaling + latent_offset).astype(jnp.bfloat16)


def unpatch(latent_rows, token_rows, token_cols, channels):
    shaped = latent_rows.reshape(token_rows, token_cols, channels, 2, 2)
    return jnp.transpose(shaped, (0, 3, 1, 4, 2)).reshape(2 * token_rows, 2 * token_cols, channels)


def conv_apply(padded, convolution_kernel, convolution_bias):
    height = padded.shape[0] - 2
    breadth = padded.shape[1] - 2
    shifted = [
        padded[row_step : row_step + height, col_step : col_step + breadth]
        for row_step in range(3)
        for col_step in range(3)
    ]
    stacked = jnp.concatenate(shifted, axis=2).reshape(height * breadth, -1)
    flat_weight = convolution_kernel.reshape(-1, convolution_kernel.shape[3])
    output = jnp.dot(stacked, flat_weight, preferred_element_type=jnp.float32) + convolution_bias
    return output.reshape(height, breadth, -1).astype(jnp.bfloat16)


def on_device(
    queries,
    head_keys,
    head_values,
    region_request,
    request_adapter,
    residual,
    output_gate,
    output_weight,
    adapter_down_factors,
    adapter_up_factors,
    closing_scale,
    closing_shift,
    patch_projection_weight,
    patch_projection_bias,
    convolution_kernel,
    convolution_bias,
):
    query_group, key_group, value_group = (
        lax.all_to_all(queries, "tile", split_axis=1, concat_axis=0, tiled=True),
        lax.all_to_all(head_keys, "tile", split_axis=1, concat_axis=0, tiled=True),
        lax.all_to_all(head_values, "tile", split_axis=1, concat_axis=0, tiled=True),
    )
    group_rows = query_group.shape[0]
    local_heads = query_group.shape[1] // HD
    width_here = key_group.shape[1]
    paired = jnp.concatenate([key_group, value_group], axis=1)
    framed_pairs = with_halo(paired, (("seq", 0),), WIN)
    key_heads = framed_pairs[:, :width_here].reshape(-1, local_heads, HD)
    value_heads = framed_pairs[:, width_here:].reshape(-1, local_heads, HD)
    token_total = group_rows * lax.axis_size("seq")
    first_token = lax.axis_index("seq") * group_rows
    attended_heads = band_attention(
        query_group.reshape(group_rows, local_heads, HD),
        key_heads,
        value_heads,
        first_token,
        token_total,
        WIN,
        HD,
    )
    token_attended = lax.all_to_all(attended_heads, "tile", split_axis=0, concat_axis=1, tiled=True)
    adapter_list = adapter_of(region_request, request_adapter)
    lowered_result = reduced_rank(token_attended, adapter_down_factors, adapter_list, ADAPTER_RANK)
    weight_slice, up_factor_slice = lax.all_gather(
        (output_weight, adapter_up_factors), "tile", axis=1, tiled=True
    )
    branch_output = jnp.dot(
        token_attended, weight_slice, preferred_element_type=jnp.float32
    ) + jnp.dot(lowered_result, up_factor_slice, preferred_element_type=jnp.float32)
    block_out = lax.optimization_barrier(
        (residual.astype(jnp.float32) + output_gate * branch_output).astype(jnp.bfloat16)
    )
    latents = patch_latents(
        block_out, closing_scale, closing_shift, patch_projection_weight, patch_projection_bias
    )
    strip_rows = lax.all_gather(latents, "tile", axis=0, tiled=True)
    token_rows = strip_rows.shape[0] // LAT_W
    pixels = unpatch(strip_rows, token_rows, LAT_W, LAT_CH)
    slab_width = 2 * LAT_W // lax.axis_size("tile")
    widened = jnp.pad(pixels, ((0, 0), (1, 1), (0, 0)))
    column_start = lax.axis_index("tile") * slab_width
    column_slab = lax.dynamic_slice_in_dim(widened, column_start, slab_width + 2, 1)
    framed = with_halo(column_slab, (("seq", 0),), 1)
    return conv_apply(framed, convolution_kernel, convolution_bias)


def solution(mesh):
    return jax.shard_map(
        on_device,
        mesh=mesh,
        in_specs=(
            P(("seq", "tile"), None),
            P(("seq", "tile"), None),
            P(("seq", "tile"), None),
            P(("seq", "tile")),
            P(),
            P(("seq", "tile"), None),
            P(),
            P(None, "tile"),
            P(),
            P(None, "tile"),
            P(),
            P(),
            P(),
            P(),
            P(),
            P(),
        ),
        out_specs=P("seq", "tile", None),
        check_vma=False,
    )
```

profile of v0, /device:TPU:1, one launch (start us, length us, event | category | flops | bytes accessed | tf_op | source)
XLA Modules:
  0.0 428.5 jit_solution(8271147297495345797)
XLA Ops:
  7.3 2.0 copy_bitcast_fusion
  9.3 9.2 %all-to-all-start.1 = ((bf16[128,16,128]{2,0,1:T(8,128)(2,1)}), bf16[128,16,128]{2,0,1:T(8,128)(2,1)S(1)}, u32[]{:S(2)}, u32[]{:S(2)}) async-start(bf16[128,16,128]{2,0,1:T(8,128)(2,1)} %copy_bitcast_fusion), calls=%async_computation.1 | async-start | bytes 1048576 | tf_op jit(solution)/shard_map/all_to_all | solution.py:145
  19.5 14.7 %all-to-all-done.1 = bf16[128,16,128]{2,0,1:T(8,128)(2,1)S(1)} async-done(((bf16[128,16,128]{2,0,1:T(8,128)(2,1)}), bf16[128,16,128]{2,0,1:T(8,128)(2,1)S(1)}, u32[]{:S(2)}, u32[]{:S(2)}) %all-to-all-start.1) | async-done | bytes 524320 | tf_op jit(solution)/shard_map/all_to_all | solution.py:145
  34.2 3.6 all-to-all-start
  38.9 27.4 %all-to-all-done = bf16[128,16,128]{2,0,1:T(8,128)(2,1)S(1)} async-done(((bf16[128,16,128]{2,0,1:T(8,128)(2,1)}), bf16[128,16,128]{2,0,1:T(8,128)(2,1)S(1)}, u32[]{:S(2)}, u32[]{:S(2)}) %all-to-all-start) | async-done | bytes 524320 | tf_op jit(solution)/shard_map/all_to_all | solution.py:144
  66.3 4.6 %all-to-all-start.2 = ((bf16[128,16,128]{0,2,1:T(8,128)(2,1)}), bf16[128,16,128]{0,2,1:T(8,128)(2,1)S(1)}, u32[]{:S(2)}, u32[]{:S(2)}) async-start(bf16[128,16,128]{0,2,1:T(8,128)(2,1)} %bitcast.12), calls=%async_computation.2 | async-start | bytes 1048576 | tf_op jit(solution)/shard_map/all_to_all | solution.py:143
  71.7 13.8 %collective-permute-start = (bf16[512,256]{1,0:T(8,128)(2,1)}, bf16[512,256]{1,0:T(8,128)(2,1)S(1)}, u32[]{:S(2)}, u32[]{:S(2)}) collective-permute-start(bf16[512,256]{1,0:T(8,128)(2,1)} %get-tuple-element.121), channel_id=1, source_target_pairs={{0,16},{16,32},{32,48},{48,64},{64,80},{80,96},{96,112},{112,128},... | collective-permute-start | bytes 786440 | tf_op jit(solution)/shard_map/ppermute | solution.py:25
  85.5 1.9 collective-permute-start.1
  87.4 15.9 %all-to-all-done.2 = bf16[128,16,128]{0,2,1:T(8,128)(2,1)S(1)} async-done(((bf16[128,16,128]{0,2,1:T(8,128)(2,1)}), bf16[128,16,128]{0,2,1:T(8,128)(2,1)S(1)}, u32[]{:S(2)}, u32[]{:S(2)}) %all-to-all-start.2) | async-done | bytes 524320 | tf_op jit(solution)/shard_map/all_to_all | solution.py:143
  104.0 19.4 %while.12 = (s32[]{:T(128)}, bf16[4,512,1,128]{3,1,0,2:T(8,128)(2,1)}, s32[4]{0:T(128)S(1)}, bf16[3072,1,128]{2,0,1:T(8,128)(2,1)S(1)}, s32[]{:T(128)}, /*index=...) while((s32[]{:T(128)}, ...), condition=%wide.region_3.4_spmd, body=%wide.region_0.3_spmd.sunk | while | flops 412227072 | bytes 11046656 | solution.py:65
  105.2 1.5 fusion.78
  110.1 1.5 fusion.78
  114.9 1.5 fusion.78
  119.8 1.5 fusion.78
  123.4 33.3 %all-to-all-start.3 = ((bf16[16,128,128]{2,1,0:T(8,128)(2,1)}), bf16[16,128,128]{2,1,0:T(8,128)(2,1)S(1)}, u32[]{:S(2)}, u32[]{:S(2)}) async-start(bf16[16,128,128]{2,1,0:T(8,128)(2,1)} %bitcast.16), calls=%async_computation.3 | async-start | bytes 1048576 | tf_op jit(solution)/shard_map/all_to_all | solution.py:165
  156.9 72.6 %all_gather.10 = bf16[128,3072]{0,1:T(8,128)(2,1)} all-gather(bf16[128,192]{0,1:T(8,128)(2,1)S(1)} %copy-done.3), channel_id=1, replica_groups=mesh['seq'=32,'tile'=16] {'tile'}, dimensions={1}, use_global_device_ids=true | all-gather | bytes 835584 | tf_op jit(solution)/shard_map/all_gather | solution.py:168
  229.8 110.2 %all-gather.2.cloned.1.call-done = bf16[2048,3072]{0,1:T(8,128)(2,1)} async-done(((bf16[2048,192]{0,1:T(8,128)(2,1)}), bf16[2048,3072]{0,1:T(8,128)(2,1)}) %all-gather.2.cloned.1.call-update) | async-done | bytes 12582928 | tf_op jit(solution)/shard_map/all_gather | solution.py:168
  340.0 8.9 %fusion.58 = f32[128,3072]{1,0:T(8,128)S(1)} fusion(bf16[128,2048]{0,1:T(8,128)(2,1)S(1)} %bitcast.86, bf16[2048,3072]{0,1:T(8,128)(2,1)} %all-gather.2.cloned.1.call-done), kind=kOutput, calls=%fused_computation.92 | convolution fusion | flops 1610612736 | bytes 14680064 | tf_op jit(solution)/shard_map/dot_general | solution.py:171
  349.0 2.1 fusion.32
  351.6 1.6 fusion.43
  353.2 39.1 %all_gather.11 = bf16[2048,64]{0,1:T(8,128)(2,1)S(1)} all-gather(bf16[128,64]{0,1:T(8,128)(2,1)S(1)} %fusion.43), channel_id=1, replica_groups=mesh['seq'=32,'tile'=16] {'tile'}, dimensions={0}, use_global_device_ids=true | all-gather | bytes 278528 | tf_op jit(solution)/shard_map/all_gather | solution.py:180
  393.6 17.3 %collective-permute-start.2 = (bf16[1,34,16]{2,1,0:T(8,128)(2,1)S(1)}, bf16[1,34,16]{2,1,0:T(8,128)(2,1)S(1)}, u32[]{:S(2)}, u32[]{:S(2)}) collective-permute-start(bf16[1,34,16]{2,1,0:T(8,128)(2,1)S(1)} %get-tuple-element.115), channel_id=1, source_target_pairs={{0,16},{16,32},{32,48},{48,64},{64,80},{80,96},{96,112},{112,128},... | collective-permute-start | bytes 3272 | tf_op jit(solution)/shard_map/ppermute | solution.py:25
  411.0 1.9 collective-permute-start.3
  413.2 6.7 %collective-permute-done.3 = bf16[1,34,16]{2,1,0:T(8,128)(2,1)S(1)} collective-permute-done((bf16[1,34,16]{2,1,0:T(8,128)(2,1)S(1)}, bf16[1,34,16]{2,1,0:T(8,128)(2,1)S(1)}, u32[]{:S(2)}, u32[]{:S(2)}) %collective-permute-start.3) | collective-permute-done | bytes 1120 | tf_op jit(solution)/shard_map/ppermute | solution.py:28
  (86 shorter events, 19.4 us)
Async XLA Ops:
  6.5 342.4 %copy-start = (bf16[2048,128]{1,0:T(8,128)(2,1)S(1)}, bf16[2048,128]{1,0:T(8,128)(2,1)}, u32[]{:S(2)}) copy-start(bf16[2048,128]{1,0:T(8,128)(2,1)} %param.26) | copy-start | bytes 1572868
  6.5 12.0 %copy-start.1 = (bf16[128,2048]{1,0:T(8,128)(2,1)S(1)}, bf16[128,2048]{1,0:T(8,128)(2,1)}, u32[]{:S(2)}) copy-start(bf16[128,2048]{1,0:T(8,128)(2,1)} %param.19) | copy-start | bytes 1572868
  6.5 333.5 %all-gather.2.cloned.1.call-start = ((), (), s32[]{:S(2)}) async-start(), calls=%async_computation.4 | async-start | bytes 13369344 | tf_op jit(solution)/shard_map/all_gather | solution.py:168
  7.3 30.5 %copy-start.2 = (bf16[128,2048]{1,0:T(8,128)(2,1)S(1)}, bf16[128,2048]{1,0:T(8,128)(2,1)}, u32[]{:S(2)}) copy-start(bf16[128,2048]{1,0:T(8,128)(2,1)} %param.18) | copy-start | bytes 1572868
  9.3 24.9 %all-to-all-start.1 = ((bf16[128,16,128]{2,0,1:T(8,128)(2,1)}), bf16[128,16,128]{2,0,1:T(8,128)(2,1)S(1)}, u32[]{:S(2)}, u32[]{:S(2)}) async-start(bf16[128,16,128]{2,0,1:T(8,128)(2,1)} %copy_bitcast_fusion), calls=%async_computation.1 | async-start | bytes 1048576 | tf_op jit(solution)/shard_map/all_to_all | solution.py:145
  34.2 32.0 %all-to-all-start = ((bf16[128,16,128]{2,0,1:T(8,128)(2,1)}), bf16[128,16,128]{2,0,1:T(8,128)(2,1)S(1)}, u32[]{:S(2)}, u32[]{:S(2)}) async-start(bf16[128,16,128]{2,0,1:T(8,128)(2,1)} %copy_bitcast_fusion.1), calls=%async_computation | async-start | bytes 1048576 | tf_op jit(solution)/shard_map/all_to_all | solution.py:144
  66.3 37.1 %all-to-all-start.2 = ((bf16[128,16,128]{0,2,1:T(8,128)(2,1)}), bf16[128,16,128]{0,2,1:T(8,128)(2,1)S(1)}, u32[]{:S(2)}, u32[]{:S(2)}) async-start(bf16[128,16,128]{0,2,1:T(8,128)(2,1)} %bitcast.12), calls=%async_computation.2 | async-start | bytes 1048576 | tf_op jit(solution)/shard_map/all_to_all | solution.py:143
  71.7 32.0 %collective-permute-start = (bf16[512,256]{1,0:T(8,128)(2,1)}, bf16[512,256]{1,0:T(8,128)(2,1)S(1)}, u32[]{:S(2)}, u32[]{:S(2)}) collective-permute-start(bf16[512,256]{1,0:T(8,128)(2,1)} %get-tuple-element.121), channel_id=1, source_target_pairs={{0,16},{16,32},{32,48},{48,64},{64,80},{80,96},{96,112},{112,128},... | collective-permute-start | bytes 786440 | tf_op jit(solution)/shard_map/ppermute | solution.py:25
  85.5 18.2 %collective-permute-start.1 = (bf16[512,256]{1,0:T(8,128)(2,1)S(1)}, bf16[512,256]{1,0:T(8,128)(2,1)S(1)}, u32[]{:S(2)}, u32[]{:S(2)}) collective-permute-start(bf16[512,256]{1,0:T(8,128)(2,1)S(1)} %get-tuple-element.122), channel_id=1, source_target_pairs={{16,0},{32,16},{48,32},{64,48},{80,64},{96,80},{112,96},{128,112},... | collective-permute-start | bytes 786440 | tf_op jit(solution)/shard_map/ppermute | solution.py:28
  103.9 52.8 %copy-start.9 = (s32[8]{0:T(128)S(1)}, s32[8]{0:T(128)}, u32[]{:S(2)}) copy-start(s32[8]{0:T(128)} %param.22) | copy-start | bytes 100
  104.0 52.8 %copy-start.10 = (s32[128]{0:T(128)S(1)}, s32[128]{0:T(128)}, u32[]{:S(2)}) copy-start(s32[128]{0:T(128)} %param.21) | copy-start | bytes 1540
  104.0 52.9 %copy-start.5 = (f32[3072]{0:T(1024)S(1)}, f32[3072]{0:T(1024)}, u32[]{:S(2)}) copy-start(f32[3072]{0:T(1024)} %param.28) | copy-start | bytes 36868
  104.0 52.9 %copy-start.3 = (bf16[128,192]{0,1:T(8,128)(2,1)S(1)}, bf16[128,192]{0,1:T(8,128)(2,1)}, u32[]{:S(2)}) copy-start(bf16[128,192]{0,1:T(8,128)(2,1)} %param.27) | copy-start | bytes 147460
  123.4 106.0 %all-to-all-start.3 = ((bf16[16,128,128]{2,1,0:T(8,128)(2,1)}), bf16[16,128,128]{2,1,0:T(8,128)(2,1)S(1)}, u32[]{:S(2)}, u32[]{:S(2)}) async-start(bf16[16,128,128]{2,1,0:T(8,128)(2,1)} %bitcast.16), calls=%async_computation.3 | async-start | bytes 1048576 | tf_op jit(solution)/shard_map/all_to_all | solution.py:165
  340.0 8.9 %copy-start.4 = (f32[3072]{0:T(1024)S(1)}, f32[3072]{0:T(1024)}, u32[]{:S(2)}) copy-start(f32[3072]{0:T(1024)} %param.24) | copy-start | bytes 36868
  348.9 2.7 copy-start.7
  348.9 2.7 copy-start.11
  393.6 19.6 %collective-permute-start.2 = (bf16[1,34,16]{2,1,0:T(8,128)(2,1)S(1)}, bf16[1,34,16]{2,1,0:T(8,128)(2,1)S(1)}, u32[]{:S(2)}, u32[]{:S(2)}) collective-permute-start(bf16[1,34,16]{2,1,0:T(8,128)(2,1)S(1)} %get-tuple-element.115), channel_id=1, source_target_pairs={{0,16},{16,32},{32,48},{48,64},{64,80},{80,96},{96,112},{112,128},... | collective-permute-start | bytes 3272 | tf_op jit(solution)/shard_map/ppermute | solution.py:25
  411.0 8.9 %collective-permute-start.3 = (bf16[1,34,16]{2,1,0:T(8,128)(2,1)S(1)}, bf16[1,34,16]{2,1,0:T(8,128)(2,1)S(1)}, u32[]{:S(2)}, u32[]{:S(2)}) collective-permute-start(bf16[1,34,16]{2,1,0:T(8,128)(2,1)S(1)} %get-tuple-element.114), channel_id=1, source_target_pairs={{16,0},{32,16},{48,32},{64,48},{80,64},{96,80},{112,96},{128,112},... | collective-permute-start | bytes 3272 | tf_op jit(solution)/shard_map/ppermute | solution.py:28
  413.1 7.5 %copy-start.6 = (bf16[3,3,16,512]{3,2,1,0:T(8,128)(2,1)S(1)}, bf16[3,3,16,512]{3,2,1,0:T(8,128)(2,1)}, u32[]{:S(2)}) copy-start(bf16[3,3,16,512]{3,2,1,0:T(8,128)(2,1)} %param.32) | copy-start | bytes 442372
  413.1 7.5 %copy-start.8 = (f32[512]{0:T(512)S(1)}, f32[512]{0:T(512)}, u32[]{:S(2)}) copy-start(f32[512]{0:T(512)} %param.33) | copy-start | bytes 6148
Sparse Core Ops, SparseCore 0:
  9.4 330.5 all-gather.1
where the time goes:
time: 429 us
  waiting for transfers between devices  176 us (41%)
  blocking collectives  112 us (26%)
  starting transfers between devices  85.7 us (20%)
  matrix products  22.6 us (5%)
  between operations  13.8 us (3%)
  local copies, waits for them, and re-layouts  12.5 us (3%)
    all_gather x1, waiting for transfers between devices, on_device(): lax.all_gather((output_weight, adapter_up_factors), 'tile', axis=1, tiled...  110 us
    all_gather x1, blocking collectives, on_device(): lax.all_gather((output_weight, adapter_up_factors), 'tile', axis=1, tiled...  72.6 us
    all_gather x1, blocking collectives, on_device(): strip_rows = lax.all_gather(latents, 'tile', axis=0, tiled=True)  39.1 us
    all_to_all x1, starting transfers between devices, on_device(): lax.all_to_all(attended_heads, 'tile', split_axis=0, concat_axis=1, tiled...  33.3 us
    ppermute x2, starting transfers between devices, with_halo(): lax.ppermute(lax.slice_in_dim(block, block.shape[dim] - width, None, axis...  31.2 us
    all_to_all x1, waiting for transfers between devices, on_device(): lax.all_to_all(head_keys, 'tile', split_axis=1, concat_axis=0, tiled=True)  27.4 us
    all_to_all x1, waiting for transfers between devices, on_device(): lax.all_to_all(queries, 'tile', split_axis=1, concat_axis=0, tiled=True)  15.9 us
    all_to_all x1, waiting for transfers between devices, on_device(): lax.all_to_all(head_values, 'tile', split_axis=1, concat_axis=0, tiled=True)  14.7 us
  transfers between devices with their start and end apart: 9, of which 5 were waited for; matrix products, arithmetic and copies ran while one was open for 5% of the time, Pallas kernels for 0%

commit v1 on v0

v1 whole, which is shorter than its diff:
```python
import math

import jax
import jax.numpy as jnp
from jax import lax
from jax.experimental import pallas as pl
from jax.experimental.pallas import tpu as pltpu
from jax.sharding import PartitionSpec as P

HD = 128
WIN = 512
SEQ = 32
TILE = 16
BLOCK = 128
BAND = 2048
FEATS = 2048
WIDTH = 3072
QUARTER = WIDTH // 4
SHARD = WIDTH // TILE
RANKS = 128
DEEP = FEATS + RANKS
EIGHTH = DEEP // 8
KEYS = BLOCK + 2 * WIN

norm_epsilon = 1e-06
latent_scaling = 0.3611
latent_offset = 0.1159

MESH = pl.DeviceIdType.MESH
F32 = jnp.float32
BF16 = jnp.bfloat16


def wait_bytes(ref, sem):
    pltpu.make_async_copy(ref, ref, sem).wait()


def kernel(
    q_hbm,
    k_hbm,
    v_hbm,
    request,
    request_adapter,
    residual_hbm,
    gate,
    weight_hbm,
    down,
    up_hbm,
    scale,
    shift,
    patch_weight,
    patch_bias,
    conv_kernel,
    conv_bias,
    out,
    qbuf,
    kbuf,
    vbuf,
    att,
    wraw,
    wq,
    rbuf,
    mbuf,
    gbuf,
    xbuf,
    msg,
    msgin,
    lat,
    lbuf,
    lfull,
    wc,
    obuf,
    bias_row,
    r_qkv,
    s_qkv,
    r_halo,
    s_halo,
    l_w,
    r_w,
    s_w,
    r_res,
    s_res,
    r_g,
    s_g,
    r_y,
    s_y,
    r_msg,
    s_msg,
    r_lat,
    s_lat,
    r_lh,
    s_lh,
):
    t = lax.axis_index("tile")
    s = lax.axis_index("seq")
    y = t // 4
    z = lax.rem(t, 4)
    core = lax.rem(s, 2)
    x = s // 8
    sibling = s + 1 - 2 * core
    first = s == 0
    last = s == SEQ - 1

    def remote(src, dst, send_sem, recv_sem, where):
        return pltpu.make_async_remote_copy(
            src_ref=src,
            dst_ref=dst,
            send_sem=send_sem,
            recv_sem=recv_sem,
            device_id=where,
            device_id_type=MESH,
        )

    @pl.when(first)
    def _():
        kbuf[0:WIN, :] = jnp.zeros((WIN, HD), BF16)
        vbuf[0:WIN, :] = jnp.zeros((WIN, HD), BF16)
        lbuf[0] = jnp.zeros((48, 128), BF16)

    @pl.when(last)
    def _():
        kbuf[WIN + BAND :, :] = jnp.zeros((WIN, HD), BF16)
        vbuf[WIN + BAND :, :] = jnp.zeros((WIN, HD), BF16)
        lbuf[9] = jnp.zeros((48, 128), BF16)

    @pl.when(t == 0)
    def _():
        lbuf[1:9, 0:16, :] = jnp.zeros((8, 16, 128), BF16)

    @pl.when(t == TILE - 1)
    def _():
        lbuf[1:9, 32:48, :] = jnp.zeros((8, 16, 128), BF16)

    barrier = pltpu.get_barrier_semaphore()

    def greet(d, carry):
        pl.semaphore_signal(
            barrier, inc=1, device_id={"tile": lax.rem(t + d, TILE)}, device_id_type=MESH
        )
        return carry

    lax.fori_loop(1, TILE, greet, 0)
    for d in range(1, 4):
        pl.semaphore_signal(
            barrier, inc=1, device_id={"seq": lax.rem(s + 8 * d, SEQ)}, device_id_type=MESH
        )

    @pl.when(jnp.logical_not(first))
    def _():
        pl.semaphore_signal(barrier, inc=1, device_id={"seq": s - 1}, device_id_type=MESH)

    @pl.when(jnp.logical_not(last))
    def _():
        pl.semaphore_signal(barrier, inc=1, device_id={"seq": s + 1}, device_id_type=MESH)

    w_local = pltpu.make_async_copy(weight_hbm, wraw.at[z, pl.ds(0, FEATS), :], l_w.at[0])
    u_local = pltpu.make_async_copy(up_hbm, wraw.at[z, pl.ds(FEATS, RANKS), :], l_w.at[1])
    w_local.start()
    u_local.start()

    pl.semaphore_wait(
        barrier, TILE - 1 + 3 + jnp.where(first, 0, 1) + jnp.where(last, 0, 1)
    )

    own_rows = pl.ds(pl.multiple_of(WIN + t * BLOCK, BLOCK), BLOCK)
    own_q_rows = pl.ds(pl.multiple_of(t * BLOCK, BLOCK), BLOCK)
    sets = ((k_hbm, kbuf, own_rows), (v_hbm, vbuf, own_rows), (q_hbm, qbuf, own_q_rows))
    for a, (src, dst, rows) in enumerate(sets):

        def send(d, carry, a=a, src=src, dst=dst, rows=rows):
            p = lax.rem(t + d, TILE)
            cols = pl.ds(pl.multiple_of(p * HD, HD), HD)
            remote(
                src.at[:, cols], dst.at[rows, :], s_qkv.at[a], r_qkv.at[a, y], {"tile": p}
            ).start()
            return carry

        lax.fori_loop(1, TILE, send, 0)
        own_cols = pl.ds(pl.multiple_of(t * HD, HD), HD)
        pltpu.make_async_copy(src.at[:, own_cols], dst.at[rows, :], r_qkv.at[a, y]).start()

    adapters = jnp.zeros((1, BLOCK), jnp.int32)
    for r in range(8):
        adapters = adapters + jnp.where(request[...] == r, request_adapter[r], 0)
    owner = lax.broadcasted_iota(jnp.int32, (RANKS, BLOCK), 0) // 32
    kept = jnp.where(jnp.broadcast_to(adapters, (RANKS, BLOCK)) == owner, 1.0, 0.0)
    mbuf[y] = kept.T.astype(BF16)

    for d in range(4):
        y2 = lax.rem(y + d, 4)
        cols = pl.ds(pl.multiple_of(y2 * QUARTER, 128), QUARTER)
        if d == 0:
            pltpu.make_async_copy(residual_hbm.at[:, cols], rbuf.at[y], r_res.at[0]).start()
        else:
            where = {"tile": y2 * 4 + z}
            remote(
                residual_hbm.at[:, cols], rbuf.at[y], s_res.at[0], r_res.at[0], where
            ).start()
            remote(mbuf.at[y], mbuf.at[y], s_res.at[1], r_res.at[1], where).start()

    w_local.wait()
    u_local.wait()
    e_rows = pl.ds(pl.multiple_of((core * 4 + x) * EIGHTH, 16), EIGHTH)
    half_rows = pl.ds(pl.multiple_of(core * 4 * EIGHTH, 16), 4 * EIGHTH)
    for d in range(1, 4):
        z2 = lax.rem(z + d, 4)
        remote(
            wraw.at[z, e_rows, :],
            wraw.at[z, e_rows, :],
            s_w.at[0],
            r_w.at[0],
            {"tile": y * 4 + z2},
        ).start()

    flat_kernel = conv_kernel[...].reshape(144, 512)
    place = lax.broadcasted_iota(jnp.int32, (512, 144), 0)
    tap = lax.broadcasted_iota(jnp.int32, (512, 144), 1)
    lane = lax.rem(place, 128)
    dri = place // 256
    dwi = lax.rem(place // 128, 2)
    pa = lax.rem(lane // 2, 2)
    pb = lax.rem(lane, 2)
    for a in range(2):
        for b in range(2):
            ky = 2 * dri + a + pa - 1
            kx = 2 * dwi + b + pb - 1
            good = (
                (lane < 64)
                & (ky >= 0)
                & (ky < 3)
                & (kx >= 0)
                & (kx < 3)
                & (tap == (ky * 3 + kx) * 16 + lane // 4)
            )
            pick = jnp.where(good, 1.0, 0.0).astype(BF16)
            wc[2 * a + b] = jnp.dot(pick, flat_kernel, preferred_element_type=F32).astype(BF16)
    bias_row[...] = jnp.zeros((8, 128), F32)
    bias_row[0:1, 0:64] = patch_bias[...]

    wait_bytes(wraw.at[pl.ds(0, 3), pl.ds(0, EIGHTH), :], r_w.at[0])
    for d in range(1, 4):
        z2 = lax.rem(z + d, 4)
        for e in range(1, 4):
            remote(
                wraw.at[z2, e_rows, :],
                wraw.at[z2, e_rows, :],
                s_w.at[1],
                r_w.at[1],
                {"seq": lax.rem(s + 8 * e, SEQ)},
            ).start()

    for row in (3, 0):
        for a in range(2):
            buf = (kbuf, vbuf)[a]
            wait_bytes(buf.at[pl.ds(WIN, 4 * BLOCK), :], r_qkv.at[a, row])

    def halo(buf, a, up):
        if up:
            src = buf.at[pl.ds(WIN + 3 * WIN, WIN), :]
            dst = buf.at[pl.ds(0, WIN), :]
            return remote(src, dst, s_halo.at[0], r_halo.at[0], {"seq": s + 1})
        src = buf.at[pl.ds(WIN, WIN), :]
        dst = buf.at[pl.ds(WIN + BAND, WIN), :]
        return remote(src, dst, s_halo.at[1], r_halo.at[1], {"seq": s - 1})

    @pl.when(jnp.logical_not(last))
    def _():
        halo(kbuf, 0, True).start()
        halo(vbuf, 1, True).start()

    @pl.when(jnp.logical_not(first))
    def _():
        halo(kbuf, 0, False).start()
        halo(vbuf, 1, False).start()

    for row in (1, 2):
        for a in range(2):
            buf = (kbuf, vbuf)[a]
            wait_bytes(buf.at[pl.ds(WIN, 4 * BLOCK), :], r_qkv.at[a, row])
    for row in range(4):
        wait_bytes(qbuf.at[pl.ds(0, 4 * BLOCK), :], r_qkv.at[2, row])

    factor = math.log2(math.e) / math.sqrt(HD)
    row_at = lax.broadcasted_iota(jnp.int32, (BLOCK, BLOCK), 0)
    col_at = lax.broadcasted_iota(jnp.int32, (BLOCK, BLOCK), 1)

    def attend(row):
        edge = (first & (row == 0)) | (last & (row == 3))

        def block(b, edged):
            start = pl.multiple_of(row * WIN + b * BLOCK, BLOCK)
            q = qbuf[pl.ds(start, BLOCK), :]
            k = kbuf[pl.ds(start, KEYS), :]
            v = vbuf[pl.ds(start, KEYS), :]
            scores = lax.dot_general(
                q, k, (((1,), (1,)), ((), ())), preferred_element_type=F32
            )
            low = jnp.where(col_at >= row_at, scores[:, :BLOCK], -jnp.inf)
            high = jnp.where(col_at <= row_at, scores[:, KEYS - BLOCK :], -jnp.inf)
            scores = jnp.concatenate([low, scores[:, BLOCK : KEYS - BLOCK], high], axis=1)
            if edged:
                key_at = start + lax.broadcasted_iota(jnp.int32, (BLOCK, KEYS), 1)
                least = jnp.where(first, WIN, 0)
                most = jnp.where(last, WIN + BAND, 2 * WIN + BAND)
                scores = jnp.where((key_at >= least) & (key_at < most), scores, -jnp.inf)
            highest = jnp.max(scores, axis=1, keepdims=True)
            expons = jnp.exp2((scores - highest) * factor)
            totals = jnp.sum(expons, axis=1, keepdims=True)
            weighted = jnp.dot(expons.astype(BF16), v, preferred_element_type=F32)
            att[row, b] = (weighted / totals).astype(BF16)

        @pl.when(edge)
        def _():
            for b in range(4):
                block(b, True)

        @pl.when(jnp.logical_not(edge))
        def _():
            for b in range(4):
                block(b, False)

    head_cols = pl.ds(pl.multiple_of(t * HD, HD), HD)

    def send_heads(row):
        pltpu.make_async_copy(
            att.at[row, z], gbuf.at[row, :, head_cols], r_g.at[row]
        ).start()
        for d in range(1, 4):
            z2 = lax.rem(z + d, 4)
            remote(
                att.at[row, z2],
                gbuf.at[row, :, head_cols],
                s_g.at[0],
                r_g.at[row],
                {"tile": y * 4 + z2},
            ).start()

    y_up = {"tile": lax.rem(y + 1, 4) * 4 + z}
    y_down = {"tile": lax.rem(y + 3, 4) * 4 + z}

    def group_cols(which, offset=0, width=512):
        at = lax.rem(y + which, 4) * 512 + offset
        return pl.ds(pl.multiple_of(at, 128), width)

    def send_group(row):
        cols = group_cols(0)
        wait_bytes(gbuf.at[row, :, pl.ds(0, 512)], r_g.at[row])
        ref = gbuf.at[row, :, cols]
        remote(ref, ref, s_y.at[0], r_y.at[0, row], y_up).start()
        remote(ref, ref, s_y.at[0], r_y.at[1, row], y_down).start()

    def pass_on(row):
        wait_bytes(gbuf.at[row, :, pl.ds(0, 512)], r_y.at[0, row])
        ref = gbuf.at[row, :, group_cols(3, 0, 256)]
        remote(ref, ref, s_y.at[1], r_y.at[2, row], y_up).start()
        wait_bytes(gbuf.at[row, :, pl.ds(0, 512)], r_y.at[1, row])
        ref = gbuf.at[row, :, group_cols(1, 256, 256)]
        remote(ref, ref, s_y.at[1], r_y.at[3, row], y_down).start()

    row_a = jnp.where(core == 0, 3, 0)
    row_b = 3 - row_a

    def wait_halo(row):
        missing = (first & (row == 0)) | (last & (row == 3))

        @pl.when(jnp.logical_not(missing))
        def _():
            wait_bytes(kbuf.at[pl.ds(0, 2 * WIN), :], r_halo.at[jnp.where(row == 0, 0, 1)])

    attend(1)
    send_heads(1)
    attend(2)
    send_heads(2)
    send_group(1)
    wait_halo(row_a)
    attend(row_a)
    send_heads(row_a)
    send_group(2)

    wait_bytes(wraw.at[pl.ds(0, 3), pl.ds(0, 3 * EIGHTH), :], r_w.at[1])
    for d in range(1, 4):
        z2 = lax.rem(z + d, 4)
        ref = wraw.at[z2, half_rows, :]
        remote(ref, ref, s_w.at[2], r_w.at[2], {"seq": sibling}).start()

    wait_halo(row_b)
    attend(row_b)
    send_heads(row_b)
    send_group(row_a)
    pass_on(1)
    send_group(row_b)
    pass_on(2)

    wait_bytes(wraw.at[pl.ds(0, 3), pl.ds(0, 4 * EIGHTH), :], r_w.at[2])
    for c in range(DEEP // 272):
        rows = pl.ds(c * 272, 272)
        wq[rows, :] = jnp.concatenate([wraw[i, rows, :] for i in range(4)], axis=1)

    quarter = pl.ds(pl.multiple_of(y * QUARTER, 128), QUARTER)
    spread = jnp.where(
        lax.broadcasted_iota(jnp.int32, (64, 128), 0)
        == lax.broadcasted_iota(jnp.int32, (64, 128), 1),
        1.0,
        0.0,
    ).astype(BF16)
    patch_rows = pl.ds(pl.multiple_of(y * QUARTER, 128), QUARTER)
    patch = jnp.dot(patch_weight[patch_rows, :], spread, preferred_element_type=F32)
    gain = 1.0 + scale[:, quarter]
    which = lax.broadcasted_iota(jnp.int32, (8, QUARTER), 0)
    pair = jnp.where(which == 0, gain, jnp.where(which == 1, shift[:, quarter], 0.0))
    sums = jnp.dot(pair, patch, precision=lax.Precision.HIGHEST, preferred_element_type=F32)
    patch = patch.astype(BF16)

    pass_on(row_a)
    pass_on(row_b)
    for row in range(4):
        wait_bytes(gbuf.at[row, :, pl.ds(0, 256)], r_y.at[2, row])
        wait_bytes(gbuf.at[row, :, pl.ds(0, 256)], r_y.at[3, row])
    wait_bytes(rbuf, r_res.at[0])
    wait_bytes(mbuf.at[pl.ds(0, 3)], r_res.at[1])

    heads = gbuf[:, :, pl.ds(0, FEATS)].reshape(512, FEATS)
    lowered = jnp.dot(heads, down[...], preferred_element_type=F32)
    lowered = jnp.where(mbuf[...].reshape(512, RANKS) > 0, lowered, 0.0).astype(BF16)
    gbuf[:, :, pl.ds(FEATS, RANKS)] = lowered.reshape(4, BLOCK, RANKS)
    total = jnp.zeros((512, 1), F32)
    for n in range(3):
        cols = pl.ds(n * 256, 256)
        gate_cols = pl.ds(pl.multiple_of(y * QUARTER + n * 256, 128), 256)
        branch = jnp.dot(
            gbuf[...].reshape(512, DEEP), wq[:, cols], preferred_element_type=F32
        )
        base = rbuf[:, :, cols].reshape(512, 256).astype(F32)
        value = (base + gate[:, gate_cols] * branch).astype(BF16).astype(F32)
        xbuf[:, cols] = value
        total = total + jnp.sum(value, axis=1, keepdims=True)
    average = total * (1.0 / QUARTER)
    centered = xbuf[...] - average
    squares = jnp.sum(centered * centered, axis=1, keepdims=True)
    part = jnp.dot((centered * gain).astype(BF16), patch, preferred_element_type=F32)
    lane_at = lax.broadcasted_iota(jnp.int32, (512, 128), 1)
    part = jnp.where(lane_at == 64, average, jnp.where(lane_at == 65, squares, part))
    for row in range(4):
        msg[row, 0:BLOCK, :] = part[row * BLOCK : (row + 1) * BLOCK]
        msg[row, BLOCK : BLOCK + 8, :] = sums
    pltpu.make_async_copy(msg.at[y], msgin.at[y], r_msg.at[0]).start()
    for d in range(1, 4):
        y2 = lax.rem(y + d, 4)
        remote(
            msg.at[y2], msgin.at[y], s_msg.at[0], r_msg.at[0], {"tile": y2 * 4 + z}
        ).start()
    wait_bytes(msgin, r_msg.at[0])

    means = [msgin[i, 0:BLOCK, 64:65] for i in range(4)]
    spreads = [msgin[i, 0:BLOCK, 65:66] for i in range(4)]
    overall = (means[0] + means[1] + means[2] + means[3]) * 0.25
    variance = spreads[0] + spreads[1] + spreads[2] + spreads[3]
    projected = jnp.zeros((BLOCK, 128), F32)
    constant = bias_row[0:1, :]
    for i in range(4):
        off = means[i] - overall
        variance = variance + QUARTER * off * off
        projected = projected + (
            msgin[i, 0:BLOCK, :] + off * msgin[i, BLOCK : BLOCK + 1, :]
        )
        constant = constant + msgin[i, BLOCK + 1 : BLOCK + 2, :]
    projected = projected * lax.rsqrt(variance * (1.0 / WIDTH) + norm_epsilon) + constant
    latents = projected / latent_scaling + latent_offset
    small = lax.broadcasted_iota(jnp.int32, (BLOCK, 128), 1) < 64
    lat[...] = jnp.where(small, latents, 0.0).astype(BF16)

    half = lax.rem(t, 2)
    line = t // 2 + 1

    def hand(i, target, src, dst):
        far = remote(src, dst, s_lat.at[i], r_lat.at[0], {"tile": target})
        near = pltpu.make_async_copy(src, dst, r_lat.at[0])

        @pl.when(target != t)
        def _():
            far.start()

        @pl.when(target == t)
        def _():
            near.start()

        def finish():
            @pl.when(target != t)
            def _():
                far.wait_send()

        return finish

    finishes = []
    for i in range(8):
        begin = max(0, i - 1) * 16
        end = min(8, i + 2) * 16
        off = 16 if i == 0 else 0
        finishes.append(
            hand(
                i,
                half * 8 + i,
                lat.at[pl.ds(begin, end - begin), :],
                lbuf.at[line, pl.ds(off, end - begin), :],
            )
        )
    cross_src = pl.ds(pl.multiple_of(112 * (1 - half), 16), 16)
    cross_dst = pl.ds(pl.multiple_of(32 * half, 16), 16)
    finishes.append(
        hand(8, 8 - half, lat.at[cross_src, :], lbuf.at[line, cross_dst, :])
    )
    side = (t == 0) | (t == TILE - 1)

    @pl.when(side)
    def _():
        wait_bytes(lbuf.at[pl.ds(1, 8), pl.ds(0, 32), :], r_lat.at[0])

    @pl.when(jnp.logical_not(side))
    def _():
        wait_bytes(lbuf.at[pl.ds(1, 8), :, :], r_lat.at[0])

    to_next = remote(lbuf.at[8], lbuf.at[0], s_lh.at[0], r_lh.at[0], {"seq": s + 1})
    to_prev = remote(lbuf.at[1], lbuf.at[9], s_lh.at[1], r_lh.at[1], {"seq": s - 1})

    @pl.when(jnp.logical_not(last))
    def _():
        to_next.start()

    @pl.when(jnp.logical_not(first))
    def _():
        to_prev.start()

    @pl.when(jnp.logical_not(first))
    def _():
        wait_bytes(lbuf.at[0], r_lh.at[0])

    @pl.when(jnp.logical_not(last))
    def _():
        wait_bytes(lbuf.at[9], r_lh.at[1])

    lfull[...] = lbuf[...].astype(F32)
    columns = [lfull[:, 15 + i : 31 + i, :].astype(BF16) for i in range(3)]
    for a in range(2):
        for b in range(2):
            near = jnp.concatenate(
                [
                    columns[j + b][i + a : i + a + 8].reshape(128, 128)
                    for i in range(2)
                    for j in range(2)
                ],
                axis=1,
            )
            value = (
                jnp.dot(near, wc[2 * a + b], preferred_element_type=F32) + conv_bias[...]
            ).reshape(8, 16, 512)
            for r in range(8):
                for c in range(4):
                    obuf[c, 2 * r + a, pl.ds(b, 16, stride=2), :] = value[
                        r, :, c * 128 : (c + 1) * 128
                    ]
    for c in range(4):
        out[:, :, c * 128 : (c + 1) * 128] = obuf[c].astype(BF16)

    for a in range(3):
        wait_bytes(kbuf.at[pl.ds(0, 15 * BLOCK), :], s_qkv.at[a])

    @pl.when(jnp.logical_not(last))
    def _():
        wait_bytes(kbuf.at[pl.ds(0, 2 * WIN), :], s_halo.at[0])
        to_next.wait_send()

    @pl.when(jnp.logical_not(first))
    def _():
        wait_bytes(kbuf.at[pl.ds(0, 2 * WIN), :], s_halo.at[1])
        to_prev.wait_send()

    wait_bytes(wraw.at[pl.ds(0, 3), pl.ds(0, EIGHTH), :], s_w.at[0])
    wait_bytes(wraw.at[pl.ds(0, 3), pl.ds(0, 3 * EIGHTH), :], s_w.at[1])
    wait_bytes(wraw.at[pl.ds(0, 3), pl.ds(0, 4 * EIGHTH), :], s_w.at[2])
    wait_bytes(rbuf.at[pl.ds(0, 3)], s_res.at[0])
    wait_bytes(mbuf.at[pl.ds(0, 3)], s_res.at[1])
    wait_bytes(att.at[pl.ds(0, 3)], s_g.at[0])
    wait_bytes(gbuf.at[:, :, pl.ds(0, 1024)], s_y.at[0])
    wait_bytes(gbuf.at[:, :, pl.ds(0, 512)], s_y.at[1])
    wait_bytes(msg.at[pl.ds(0, 3)], s_msg.at[0])
    for finish in finishes:
        finish()


def on_device(
    queries,
    head_keys,
    head_values,
    region_request,
    request_adapter,
    residual,
    output_gate,
    output_weight,
    adapter_down_factors,
    adapter_up_factors,
    closing_scale,
    closing_shift,
    patch_projection_weight,
    patch_projection_bias,
    convolution_kernel,
    convolution_bias,
):
    far = pl.BlockSpec(memory_space=pl.ANY)
    near = pl.BlockSpec(memory_space=pltpu.VMEM)
    scalars = pl.BlockSpec(memory_space=pltpu.SMEM)
    dma = pltpu.SemaphoreType.DMA
    return pl.pallas_call(
        kernel,
        out_shape=jax.ShapeDtypeStruct((16, 32, 512), BF16),
        in_specs=[
            far, far, far, near, scalars, far, near, far,
            near, far, near, near, near, near, near, near,
        ],
        out_specs=near,
        scratch_shapes=[
            pltpu.VMEM((BAND, HD), BF16),
            pltpu.VMEM((BAND + 2 * WIN, HD), BF16),
            pltpu.VMEM((BAND + 2 * WIN, HD), BF16),
            pltpu.VMEM((4, 4, BLOCK, HD), BF16),
            pltpu.VMEM((4, DEEP, SHARD), BF16),
            pltpu.VMEM((DEEP, QUARTER), BF16),
            pltpu.VMEM((4, BLOCK, QUARTER), BF16),
            pltpu.VMEM((4, BLOCK, RANKS), BF16),
            pltpu.VMEM((4, BLOCK, DEEP), BF16),
            pltpu.VMEM((512, QUARTER), F32),
            pltpu.VMEM((4, BLOCK + 8, 128), F32),
            pltpu.VMEM((4, BLOCK + 8, 128), F32),
            pltpu.VMEM((BLOCK, 128), BF16),
            pltpu.VMEM((10, 48, 128), BF16),
            pltpu.VMEM((10, 48, 128), F32),
            pltpu.VMEM((4, 512, 512), BF16),
            pltpu.VMEM((4, 16, 32, 128), F32),
            pltpu.VMEM((8, 128), F32),
            dma((3, 4)),
            dma((3,)),
            dma((2,)),
            dma((2,)),
            dma((2,)),
            dma((3,)),
            dma((3,)),
            dma((2,)),
            dma((2,)),
            dma((4,)),
            dma((1,)),
            dma((4, 4)),
            dma((2,)),
            dma((1,)),
            dma((1,)),
            dma((1,)),
            dma((9,)),
            dma((2,)),
            dma((2,)),
        ],
        compiler_params=pltpu.CompilerParams(
            collective_id=0, has_side_effects=True, vmem_limit_bytes=48 * 1024 * 1024
        ),
    )(
        queries,
        head_keys,
        head_values,
        region_request.reshape(1, -1),
        request_adapter,
        residual,
        output_gate.reshape(1, -1),
        output_weight,
        adapter_down_factors,
        adapter_up_factors,
        closing_scale.reshape(1, -1),
        closing_shift.reshape(1, -1),
        patch_projection_weight,
        patch_projection_bias.reshape(1, -1),
        convolution_kernel,
        convolution_bias.reshape(1, -1),
    )


def solution(mesh):
    return jax.shard_map(
        on_device,
        mesh=mesh,
        in_specs=(
            P(("seq", "tile"), None),
            P(("seq", "tile"), None),
            P(("seq", "tile"), None),
            P(("seq", "tile")),
            P(),
            P(("seq", "tile"), None),
            P(),
            P(None, "tile"),
            P(),
            P(None, "tile"),
            P(),
            P(),
            P(),
            P(),
            P(),
            P(),
        ),
        out_specs=P("seq", "tile", None),
        check_vma=False,
    )
```

time: 429 us -> 131 us (0.31)
  waiting for transfers between devices: 176 us -> 0 us
  Pallas kernels: 0 us -> 122 us
  blocking collectives: 112 us -> 0 us
  starting transfers between devices: 85.7 us -> 0 us
  matrix products: 22.6 us -> 0 us
  between operations: 13.8 us -> 0.2 us
  local copies, waits for them, and re-layouts: 12.5 us -> 7.77 us
    pallas_call x0 -> x1, Pallas kernels: none -> 122 us  [on_device(): pl.pallas_call(kernel, out_shape=jax.ShapeDtypeStruct((16, 32, 512), BF16...]
    all_gather x2 -> x0, blocking collectives: 112 us -> none  [the longest x1 72.6 us: on_device(): lax.all_gather((output_weight, adapter_up_factors), 'tile', axis=1, tiled...]
    all_gather x1 -> x0, waiting for transfers between devices: 110 us -> none  [on_device(): lax.all_gather((output_weight, adapter_up_factors), 'tile', axis=1, tiled...]
    all_to_all x4 -> x0, waiting for transfers between devices: 58.1 us -> none  [the longest x1 27.4 us: on_device(): lax.all_to_all(head_keys, 'tile', split_axis=1, concat_axis=0, tiled=True)]
    all_to_all x4 -> x0, starting transfers between devices: 50.7 us -> none  [the longest x1 33.3 us: on_device(): lax.all_to_all(attended_heads, 'tile', split_axis=0, concat_axis=1, tiled...]
    ppermute x4 -> x0, starting transfers between devices: 35 us -> none  [the longest x2 31.2 us: with_halo(): lax.ppermute(lax.slice_in_dim(block, block.shape[dim] - width, None, axis...]
    dot_general x12 -> x0, matrix products: 22.6 us -> none  [the longest x1 8.91 us: on_device(): jnp.dot(token_attended, weight_slice, preferred_element_type=jnp.float32)]
    ppermute x4 -> x0, waiting for transfers between devices: 6.66 us -> none  [the longest x2 6.66 us: with_halo(): lax.ppermute(lax.slice_in_dim(block, 0, width, axis=dim), axis, backward)]
  transfers between devices with their start and end apart: 9 -> 0, of which waited for: 5 -> 0; matrix products, arithmetic and copies ran while one was open for 5% -> 0% of each run, Pallas kernels for 0% -> 0%
where the time goes in v1:
time: 131 us; the launch traced here: 130 us
  Pallas kernels  122 us (93%)
  local copies, waits for them, and re-layouts  7.77 us (6%)
    pallas_call x1, Pallas kernels, on_device(): pl.pallas_call(kernel, out_shape=jax.ShapeDtypeStruct((16, 32, 512), BF16...  122 us
    unnamed x30, local copies, waits for them, and re-layouts  7.77 us

profile of v1, /device:TPU:1, one launch (start us, length us, event | category | flops | bytes accessed | tf_op | source)
XLA Modules:
  0.0 130.0 jit_solution(2041742226945266580)
XLA Ops:
  0.0 0.9 copy.18.up_hbm
  0.9 1.4 %copy.19.patch_weight = bf16[3072,64]{1,0:T(8,128)(2,1)S(1)} copy(bf16[3072,64]{0,1:T(8,128)(2,1)} %param.28) | data formatting | bytes 786432 | tf_op args[12]
  2.3 0.0 copy-start
  2.3 0.0 copy-start.1
  2.3 0.0 copy-start.5
  2.3 0.0 copy-start.6
  2.3 0.0 copy-start.7
  2.3 0.0 copy-start.8
  2.4 0.0 copy-start.9
  2.4 0.0 copy-start.10
  2.4 0.0 copy-start.11
  2.4 0.0 copy-start.12
  2.4 1.5 %copy.17.weight_hbm = bf16[2048,192]{1,0:T(8,128)(2,1)S(1)} copy(bf16[2048,192]{0,1:T(8,128)(2,1)} %param.23) | data formatting | bytes 1572864 | tf_op args[7]
  3.9 0.0 copy-done
  3.9 0.0 copy-done.1
  4.0 0.0 copy-done.5
  4.0 0.0 copy-done.6
  4.0 0.0 copy-done.7
  4.0 0.0 copy-start.2
  4.0 1.0 copy-done.2
  5.1 1.0 copy-done.3
  6.1 1.0 copy-done.4
  7.2 122.1 %shard_map.154 = bf16[16,32,512]{2,1,0:T(8,128)(2,1)S(1)} custom-call(bf16[128,2048]{1,0:T(8,128)(2,1)S(1)} %copy-done.1, bf16[128,2048]{1,0:T(8,128)(2,1)S(1)} %copy-done.2, bf16[128,2048]{1,0:T(8,128)(2,1)S(1)} %copy-done.3, s32[1,128]{1,0:T(1,128)S(1)} %bitcast.10, s32[8]{0:T(128)S(1)} %copy-done.11, bf16[128,3072]{1,0:T(8,128)(2,1)S(1)} %copy-done, ...), custom_call_target="tpu_custom_call" | custom-call | tf_op jit(solution)/shard_map/pallas_call | solution.py:612
  129.2 0.8 copy.21
  (7 shorter events, 0.0 us)
Async XLA Ops:
  2.3 1.7 %copy-start = (bf16[128,3072]{1,0:T(8,128)(2,1)S(1)}, bf16[128,3072]{1,0:T(8,128)(2,1)}, u32[]{:S(2)}) copy-start(bf16[128,3072]{1,0:T(8,128)(2,1)} %residual_hbm.1) | copy-start | bytes 2359300
  2.3 1.7 %copy-start.1 = (bf16[128,2048]{1,0:T(8,128)(2,1)S(1)}, bf16[128,2048]{1,0:T(8,128)(2,1)}, u32[]{:S(2)}) copy-start(bf16[128,2048]{1,0:T(8,128)(2,1)} %q_hbm.1) | copy-start | bytes 1572868
  2.3 1.7 %copy-start.5 = (bf16[3,3,16,512]{3,2,1,0:T(8,128)(2,1)S(1)}, bf16[3,3,16,512]{3,2,1,0:T(8,128)(2,1)}, u32[]{:S(2)}) copy-start(bf16[3,3,16,512]{3,2,1,0:T(8,128)(2,1)} %conv_kernel.1) | copy-start | bytes 442372
  2.3 1.6 %copy-start.6 = (f32[3072]{0:T(1024)S(1)}, f32[3072]{0:T(1024)}, u32[]{:S(2)}) copy-start(f32[3072]{0:T(1024)} %param.22) | copy-start | bytes 36868
  2.3 1.6 %copy-start.7 = (f32[3072]{0:T(1024)S(1)}, f32[3072]{0:T(1024)}, u32[]{:S(2)}) copy-start(f32[3072]{0:T(1024)} %param.26) | copy-start | bytes 36868
  2.3 1.6 %copy-start.8 = (f32[3072]{0:T(1024)S(1)}, f32[3072]{0:T(1024)}, u32[]{:S(2)}) copy-start(f32[3072]{0:T(1024)} %param.27) | copy-start | bytes 36868
  2.4 1.6 %copy-start.9 = (f32[512]{0:T(512)S(1)}, f32[512]{0:T(512)}, u32[]{:S(2)}) copy-start(f32[512]{0:T(512)} %param.31) | copy-start | bytes 6148
  2.4 1.6 %copy-start.10 = (s32[128]{0:T(128)S(1)}, s32[128]{0:T(128)}, u32[]{:S(2)}) copy-start(s32[128]{0:T(128)} %param.19) | copy-start | bytes 1540
  2.4 1.6 %copy-start.11 = (s32[8]{0:T(128)S(1)}, s32[8]{0:T(128)}, u32[]{:S(2)}) copy-start(s32[8]{0:T(128)} %request_adapter.1) | copy-start | bytes 100
  2.4 1.6 %copy-start.12 = (f32[64]{0:T(128)S(1)}, f32[64]{0:T(128)}, u32[]{:S(2)}) copy-start(f32[64]{0:T(128)} %param.29) | copy-start | bytes 772
  4.0 1.0 copy-start.2
  5.1 1.0 copy-start.3
  6.1 1.0 copy-start.4

commit v2 on v1

--- a/solution.py
+++ b/solution.py
@@ -19,7 +19,9 @@
 SHARD = WIDTH // TILE
 RANKS = 128
 DEEP = FEATS + RANKS
-EIGHTH = DEEP // 8
+PAD_DEEP = 2304
+PIECE = SHARD // 4
+HALF = PAD_DEEP // 2
 KEYS = BLOCK + 2 * WIN
 
 norm_epsilon = 1e-06
@@ -57,8 +59,8 @@
     kbuf,
     vbuf,
     att,
-    wraw,
     wq,
+    patch_wide,
     rbuf,
     mbuf,
     gbuf,
@@ -88,8 +90,6 @@
     s_msg,
     r_lat,
     s_lat,
-    r_lh,
-    s_lh,
 ):
     t = lax.axis_index("tile")
     s = lax.axis_index("seq")
@@ -125,11 +125,13 @@
 
     @pl.when(t == 0)
     def _():
-        lbuf[1:9, 0:16, :] = jnp.zeros((8, 16, 128), BF16)
+        lbuf[:, 0:16, :] = jnp.zeros((10, 16, 128), BF16)
 
     @pl.when(t == TILE - 1)
     def _():
-        lbuf[1:9, 32:48, :] = jnp.zeros((8, 16, 128), BF16)
+        lbuf[:, 32:48, :] = jnp.zeros((10, 16, 128), BF16)
+
+    wq[:, DEEP:] = jnp.zeros((QUARTER, PAD_DEEP - DEEP), BF16)
 
     barrier = pltpu.get_barrier_semaphore()
 
@@ -145,22 +147,58 @@
             barrier, inc=1, device_id={"seq": lax.rem(s + 8 * d, SEQ)}, device_id_type=MESH
         )
 
+    def ring(d):
+        far = lax.rem(lax.rem(s // 2, 4) * 4 + z + d + 16, 16)
+        return {"seq": (x * 4 + far // 4) * 2 + core, "tile": y * 4 + lax.rem(far, 4)}
+
+    two = 2 - 4 * core
+    for d in (1, -1, -two):
+        pl.semaphore_signal(barrier, inc=1, device_id=ring(d), device_id_type=MESH)
+
     @pl.when(jnp.logical_not(first))
     def _():
         pl.semaphore_signal(barrier, inc=1, device_id={"seq": s - 1}, device_id_type=MESH)
+        for p in (14, 15):
+            pl.semaphore_signal(
+                barrier, inc=1, device_id={"seq": s - 1, "tile": p}, device_id_type=MESH
+            )
 
     @pl.when(jnp.logical_not(last))
     def _():
         pl.semaphore_signal(barrier, inc=1, device_id={"seq": s + 1}, device_id_type=MESH)
-
-    w_local = pltpu.make_async_copy(weight_hbm, wraw.at[z, pl.ds(0, FEATS), :], l_w.at[0])
-    u_local = pltpu.make_async_copy(up_hbm, wraw.at[z, pl.ds(FEATS, RANKS), :], l_w.at[1])
+        for p in (0, 1):
+            pl.semaphore_signal(
+                barrier, inc=1, device_id={"seq": s + 1, "tile": p}, device_id_type=MESH
+            )
+
+    bottom = (t >= TILE - 2) & jnp.logical_not(last)
+    top = (t <= 1) & jnp.logical_not(first)
+
+    own_shard = pl.ds(pl.multiple_of(z * SHARD, 64), SHARD)
+    w_local = pltpu.make_async_copy(weight_hbm, wq.at[own_shard, pl.ds(0, FEATS)], l_w.at[0])
+    u_local = pltpu.make_async_copy(up_hbm, wq.at[own_shard, pl.ds(FEATS, RANKS)], l_w.at[1])
     w_local.start()
     u_local.start()
 
     pl.semaphore_wait(
-        barrier, TILE - 1 + 3 + jnp.where(first, 0, 1) + jnp.where(last, 0, 1)
+        barrier,
+        TILE
+        + 5
+        + jnp.where(first, 0, 1)
+        + jnp.where(last, 0, 1)
+        + jnp.where(bottom, TILE, 0)
+        + jnp.where(top, TILE, 0),
     )
+
+    half_cols = pl.ds(pl.multiple_of(core * HALF, 128), HALF)
+
+    def piece(z2):
+        return wq.at[pl.ds(pl.multiple_of(z2 * SHARD + x * PIECE, 16), PIECE), half_cols]
+
+    w_local.wait()
+    u_local.wait()
+    for d in (1, -1, two):
+        remote(piece(z), piece(z), s_w.at[0], r_w.at[0], ring(d)).start()
 
     own_rows = pl.ds(pl.multiple_of(WIN + t * BLOCK, BLOCK), BLOCK)
     own_q_rows = pl.ds(pl.multiple_of(t * BLOCK, BLOCK), BLOCK)
@@ -198,19 +236,13 @@
             ).start()
             remote(mbuf.at[y], mbuf.at[y], s_res.at[1], r_res.at[1], where).start()
 
-    w_local.wait()
-    u_local.wait()
-    e_rows = pl.ds(pl.multiple_of((core * 4 + x) * EIGHTH, 16), EIGHTH)
-    half_rows = pl.ds(pl.multiple_of(core * 4 * EIGHTH, 16), 4 * EIGHTH)
+    wait_bytes(wq.at[pl.ds(0, 3 * PIECE), pl.ds(0, HALF)], r_w.at[0])
     for d in range(1, 4):
-        z2 = lax.rem(z + d, 4)
-        remote(
-            wraw.at[z, e_rows, :],
-            wraw.at[z, e_rows, :],
-            s_w.at[0],
-            r_w.at[0],
-            {"tile": y * 4 + z2},
-        ).start()
+        ref = piece(lax.rem(z + d, 4))
+        for e in range(1, 4):
+            remote(
+                ref, ref, s_w.at[1], r_w.at[1], {"seq": lax.rem(s + 8 * e, SEQ)}
+            ).start()
 
     flat_kernel = conv_kernel[...].reshape(144, 512)
     place = lax.broadcasted_iota(jnp.int32, (512, 144), 0)
@@ -237,17 +269,26 @@
     bias_row[...] = jnp.zeros((8, 128), F32)
     bias_row[0:1, 0:64] = patch_bias[...]
 
-    wait_bytes(wraw.at[pl.ds(0, 3), pl.ds(0, EIGHTH), :], r_w.at[0])
+    quarter = pl.ds(pl.multiple_of(y * QUARTER, 128), QUARTER)
+    patch_wide[0:64, :] = patch_weight[:, quarter]
+    patch_wide[64:128, :] = jnp.zeros((64, QUARTER), BF16)
+    across = (((1,), (1,)), ((), ()))
+    gain = 1.0 + scale[:, quarter]
+    which = lax.broadcasted_iota(jnp.int32, (8, QUARTER), 0)
+    pair = jnp.where(which == 0, gain, jnp.where(which == 1, shift[:, quarter], 0.0))
+    sums = lax.dot_general(
+        pair,
+        patch_wide[...].astype(F32),
+        across,
+        precision=lax.Precision.HIGHEST,
+        preferred_element_type=F32,
+    )
+
+    wait_bytes(wq.at[pl.ds(0, 9 * PIECE), pl.ds(0, HALF)], r_w.at[1])
     for d in range(1, 4):
         z2 = lax.rem(z + d, 4)
-        for e in range(1, 4):
-            remote(
-                wraw.at[z2, e_rows, :],
-                wraw.at[z2, e_rows, :],
-                s_w.at[1],
-                r_w.at[1],
-                {"seq": lax.rem(s + 8 * e, SEQ)},
-            ).start()
+        ref = wq.at[pl.ds(pl.multiple_of(z2 * SHARD, 64), SHARD), half_cols]
+        remote(ref, ref, s_w.at[2], r_w.at[2], {"seq": sibling}).start()
 
     for row in (3, 0):
         for a in range(2):
@@ -335,27 +376,12 @@
                 {"tile": y * 4 + z2},
             ).start()
 
-    y_up = {"tile": lax.rem(y + 1, 4) * 4 + z}
-    y_down = {"tile": lax.rem(y + 3, 4) * 4 + z}
-
-    def group_cols(which, offset=0, width=512):
-        at = lax.rem(y + which, 4) * 512 + offset
-        return pl.ds(pl.multiple_of(at, 128), width)
-
     def send_group(row):
-        cols = group_cols(0)
         wait_bytes(gbuf.at[row, :, pl.ds(0, 512)], r_g.at[row])
-        ref = gbuf.at[row, :, cols]
-        remote(ref, ref, s_y.at[0], r_y.at[0, row], y_up).start()
-        remote(ref, ref, s_y.at[0], r_y.at[1, row], y_down).start()
-
-    def pass_on(row):
-        wait_bytes(gbuf.at[row, :, pl.ds(0, 512)], r_y.at[0, row])
-        ref = gbuf.at[row, :, group_cols(3, 0, 256)]
-        remote(ref, ref, s_y.at[1], r_y.at[2, row], y_up).start()
-        wait_bytes(gbuf.at[row, :, pl.ds(0, 512)], r_y.at[1, row])
-        ref = gbuf.at[row, :, group_cols(1, 256, 256)]
-        remote(ref, ref, s_y.at[1], r_y.at[3, row], y_down).start()
+        ref = gbuf.at[row, :, pl.ds(pl.multiple_of(y * 512, 128), 512)]
+        for d in range(1, 4):
+            where = {"tile": lax.rem(y + d, 4) * 4 + z}
+            remote(ref, ref, s_y.at[0], r_y.at[row], where).start()
 
     row_a = jnp.where(core == 0, 3, 0)
     row_b = 3 - row_a
@@ -366,6 +392,45 @@
         @pl.when(jnp.logical_not(missing))
         def _():
             wait_bytes(kbuf.at[pl.ds(0, 2 * WIN), :], r_halo.at[jnp.where(row == 0, 0, 1)])
+
+    def project(row):
+        wait_bytes(gbuf.at[row, :, pl.ds(0, 3 * 512)], r_y.at[row])
+        lowered = jnp.dot(gbuf[row, :, pl.ds(0, FEATS)], down[...], preferred_element_type=F32)
+        lowered = jnp.where(mbuf[row] > 0, lowered, 0.0).astype(BF16)
+        gbuf[row, :, pl.ds(FEATS, RANKS)] = lowered
+        total = jnp.zeros((BLOCK, 1), F32)
+        for n in range(3):
+            cols = pl.ds(n * 256, 256)
+            gate_cols = pl.ds(pl.multiple_of(y * QUARTER + n * 256, 128), 256)
+            branch = lax.dot_general(
+                gbuf[row],
+                wq[pl.ds(n * 256, 256), pl.ds(0, DEEP)],
+                across,
+                preferred_element_type=F32,
+            )
+            base = rbuf[row, :, cols].astype(F32)
+            value = (base + gate[:, gate_cols] * branch).astype(BF16).astype(F32)
+            xbuf[:, cols] = value
+            total = total + jnp.sum(value, axis=1, keepdims=True)
+        average = total * (1.0 / QUARTER)
+        centered = xbuf[...] - average
+        squares = jnp.sum(centered * centered, axis=1, keepdims=True)
+        part = lax.dot_general(
+            (centered * gain).astype(BF16), patch_wide[...], across, preferred_element_type=F32
+        )
+        lane_at = lax.broadcasted_iota(jnp.int32, (BLOCK, 128), 1)
+        part = jnp.where(lane_at == 64, average, jnp.where(lane_at == 65, squares, part))
+        msg[row, 0:BLOCK, :] = part
+        msg[row, BLOCK : BLOCK + 8, :] = sums
+
+        @pl.when(row == y)
+        def _():
+            pltpu.make_async_copy(msg.at[row], msgin.at[y], r_msg.at[0]).start()
+
+        @pl.when(row != y)
+        def _():
+            where = {"tile": row * 4 + z}
+            remote(msg.at[row], msgin.at[y], s_msg.at[0], r_msg.at[0], where).start()
 
     attend(1)
     send_heads(1)
@@ -376,79 +441,18 @@
     attend(row_a)
     send_heads(row_a)
     send_group(2)
-
-    wait_bytes(wraw.at[pl.ds(0, 3), pl.ds(0, 3 * EIGHTH), :], r_w.at[1])
-    for d in range(1, 4):
-        z2 = lax.rem(z + d, 4)
-        ref = wraw.at[z2, half_rows, :]
-        remote(ref, ref, s_w.at[2], r_w.at[2], {"seq": sibling}).start()
-
+    wait_bytes(wq.at[pl.ds(0, 3 * SHARD), pl.ds(0, HALF)], r_w.at[2])
+    wait_bytes(rbuf, r_res.at[0])
+    wait_bytes(mbuf.at[pl.ds(0, 3)], r_res.at[1])
+    project(1)
+    send_group(row_a)
     wait_halo(row_b)
     attend(row_b)
     send_heads(row_b)
-    send_group(row_a)
-    pass_on(1)
+    project(2)
     send_group(row_b)
-    pass_on(2)
-
-    wait_bytes(wraw.at[pl.ds(0, 3), pl.ds(0, 4 * EIGHTH), :], r_w.at[2])
-    for c in range(DEEP // 272):
-        rows = pl.ds(c * 272, 272)
-        wq[rows, :] = jnp.concatenate([wraw[i, rows, :] for i in range(4)], axis=1)
-
-    quarter = pl.ds(pl.multiple_of(y * QUARTER, 128), QUARTER)
-    spread = jnp.where(
-        lax.broadcasted_iota(jnp.int32, (64, 128), 0)
-        == lax.broadcasted_iota(jnp.int32, (64, 128), 1),
-        1.0,
-        0.0,
-    ).astype(BF16)
-    patch_rows = pl.ds(pl.multiple_of(y * QUARTER, 128), QUARTER)
-    patch = jnp.dot(patch_weight[patch_rows, :], spread, preferred_element_type=F32)
-    gain = 1.0 + scale[:, quarter]
-    which = lax.broadcasted_iota(jnp.int32, (8, QUARTER), 0)
-    pair = jnp.where(which == 0, gain, jnp.where(which == 1, shift[:, quarter], 0.0))
-    sums = jnp.dot(pair, patch, precision=lax.Precision.HIGHEST, preferred_element_type=F32)
-    patch = patch.astype(BF16)
-
-    pass_on(row_a)
-    pass_on(row_b)
-    for row in range(4):
-        wait_bytes(gbuf.at[row, :, pl.ds(0, 256)], r_y.at[2, row])
-        wait_bytes(gbuf.at[row, :, pl.ds(0, 256)], r_y.at[3, row])
-    wait_bytes(rbuf, r_res.at[0])
-    wait_bytes(mbuf.at[pl.ds(0, 3)], r_res.at[1])
-
-    heads = gbuf[:, :, pl.ds(0, FEATS)].reshape(512, FEATS)
-    lowered = jnp.dot(heads, down[...], preferred_element_type=F32)
-    lowered = jnp.where(mbuf[...].reshape(512, RANKS) > 0, lowered, 0.0).astype(BF16)
-    gbuf[:, :, pl.ds(FEATS, RANKS)] = lowered.reshape(4, BLOCK, RANKS)
-    total = jnp.zeros((512, 1), F32)
-    for n in range(3):
-        cols = pl.ds(n * 256, 256)
-        gate_cols = pl.ds(pl.multiple_of(y * QUARTER + n * 256, 128), 256)
-        branch = jnp.dot(
-            gbuf[...].reshape(512, DEEP), wq[:, cols], preferred_element_type=F32
-        )
-        base = rbuf[:, :, cols].reshape(512, 256).astype(F32)
-        value = (base + gate[:, gate_cols] * branch).astype(BF16).astype(F32)
-        xbuf[:, cols] = value
-        total = total + jnp.sum(value, axis=1, keepdims=True)
-    average = total * (1.0 / QUARTER)
-    centered = xbuf[...] - average
-    squares = jnp.sum(centered * centered, axis=1, keepdims=True)
-    part = jnp.dot((centered * gain).astype(BF16), patch, preferred_element_type=F32)
-    lane_at = lax.broadcasted_iota(jnp.int32, (512, 128), 1)
-    part = jnp.where(lane_at == 64, average, jnp.where(lane_at == 65, squares, part))
-    for row in range(4):
-        msg[row, 0:BLOCK, :] = part[row * BLOCK : (row + 1) * BLOCK]
-        msg[row, BLOCK : BLOCK + 8, :] = sums
-    pltpu.make_async_copy(msg.at[y], msgin.at[y], r_msg.at[0]).start()
-    for d in range(1, 4):
-        y2 = lax.rem(y + d, 4)
-        remote(
-            msg.at[y2], msgin.at[y], s_msg.at[0], r_msg.at[0], {"tile": y2 * 4 + z}
-        ).start()
+    project(row_a)
+    project(row_b)
     wait_bytes(msgin, r_msg.at[0])
 
     means = [msgin[i, 0:BLOCK, 64:65] for i in range(4)]
@@ -472,71 +476,65 @@
     half = lax.rem(t, 2)
     line = t // 2 + 1
 
-    def hand(i, target, src, dst):
-        far = remote(src, dst, s_lat.at[i], r_lat.at[0], {"tile": target})
-        near = pltpu.make_async_copy(src, dst, r_lat.at[0])
-
-        @pl.when(target != t)
+    def hand(i, target, src, dst, shift, sending):
+        recv = r_lat.at[shift % 3]
+        if shift == 0:
+            far = remote(src, dst, s_lat.at[i], recv, {"tile": target})
+            near = pltpu.make_async_copy(src, dst, recv)
+            away = target != t
+
+            @pl.when(target == t)
+            def _():
+                near.start()
+        else:
+            where = {"seq": s + shift, "tile": target}
+            far = remote(src, dst, s_lat.at[i], recv, where)
+            away = sending
+
+        @pl.when(away)
         def _():
             far.start()
 
-        @pl.when(target == t)
-        def _():
-            near.start()
-
         def finish():
-            @pl.when(target != t)
+            @pl.when(away)
             def _():
                 far.wait_send()
 
         return finish
 
     finishes = []
-    for i in range(8):
-        begin = max(0, i - 1) * 16
-        end = min(8, i + 2) * 16
-        off = 16 if i == 0 else 0
-        finishes.append(
-            hand(
-                i,
-                half * 8 + i,
-                lat.at[pl.ds(begin, end - begin), :],
-                lbuf.at[line, pl.ds(off, end - begin), :],
-            )
-        )
     cross_src = pl.ds(pl.multiple_of(112 * (1 - half), 16), 16)
     cross_dst = pl.ds(pl.multiple_of(32 * half, 16), 16)
-    finishes.append(
-        hand(8, 8 - half, lat.at[cross_src, :], lbuf.at[line, cross_dst, :])
-    )
+    for k, (shift, sending, at) in enumerate(((1, bottom, 0), (-1, top, 9), (0, None, line))):
+        for i in range(8):
+            begin = max(0, i - 1) * 16
+            size = min(8, i + 2) * 16 - begin
+            src = lat.at[pl.ds(begin, size), :]
+            dst = lbuf.at[at, pl.ds(16 if i == 0 else 0, size), :]
+            finishes.append(hand(9 * k + i, half * 8 + i, src, dst, shift, sending))
+        src = lat.at[cross_src, :]
+        dst = lbuf.at[at, cross_dst, :]
+        finishes.append(hand(9 * k + 8, 8 - half, src, dst, shift, sending))
     side = (t == 0) | (t == TILE - 1)
 
-    @pl.when(side)
-    def _():
-        wait_bytes(lbuf.at[pl.ds(1, 8), pl.ds(0, 32), :], r_lat.at[0])
-
-    @pl.when(jnp.logical_not(side))
-    def _():
-        wait_bytes(lbuf.at[pl.ds(1, 8), :, :], r_lat.at[0])
-
-    to_next = remote(lbuf.at[8], lbuf.at[0], s_lh.at[0], r_lh.at[0], {"seq": s + 1})
-    to_prev = remote(lbuf.at[1], lbuf.at[9], s_lh.at[1], r_lh.at[1], {"seq": s - 1})
+    def wait_lines(begin, count, sem):
+        @pl.when(side)
+        def _():
+            wait_bytes(lbuf.at[pl.ds(begin, count), pl.ds(0, 32), :], sem)
+
+        @pl.when(jnp.logical_not(side))
+        def _():
+            wait_bytes(lbuf.at[pl.ds(begin, count), :, :], sem)
+
+    wait_lines(1, 8, r_lat.at[0])
+
+    @pl.when(jnp.logical_not(first))
+    def _():
+        wait_lines(0, 1, r_lat.at[1])
 
     @pl.when(jnp.logical_not(last))
     def _():
-        to_next.start()
-
-    @pl.when(jnp.logical_not(first))
-    def _():
-        to_prev.start()
-
-    @pl.when(jnp.logical_not(first))
-    def _():
-        wait_bytes(lbuf.at[0], r_lh.at[0])
-
-    @pl.when(jnp.logical_not(last))
-    def _():
-        wait_bytes(lbuf.at[9], r_lh.at[1])
+        wait_lines(9, 1, r_lat.at[2])
 
     lfull[...] = lbuf[...].astype(F32)
     columns = [lfull[:, 15 + i : 31 + i, :].astype(BF16) for i in range(3)]
@@ -567,21 +565,18 @@
     @pl.when(jnp.logical_not(last))
     def _():
         wait_bytes(kbuf.at[pl.ds(0, 2 * WIN), :], s_halo.at[0])
-        to_next.wait_send()
 
     @pl.when(jnp.logical_not(first))
     def _():
         wait_bytes(kbuf.at[pl.ds(0, 2 * WIN), :], s_halo.at[1])
-        to_prev.wait_send()
-
-    wait_bytes(wraw.at[pl.ds(0, 3), pl.ds(0, EIGHTH), :], s_w.at[0])
-    wait_bytes(wraw.at[pl.ds(0, 3), pl.ds(0, 3 * EIGHTH), :], s_w.at[1])
-    wait_bytes(wraw.at[pl.ds(0, 3), pl.ds(0, 4 * EIGHTH), :], s_w.at[2])
+
+    wait_bytes(wq.at[pl.ds(0, 3 * PIECE), pl.ds(0, HALF)], s_w.at[0])
+    wait_bytes(wq.at[pl.ds(0, 9 * PIECE), pl.ds(0, HALF)], s_w.at[1])
+    wait_bytes(wq.at[pl.ds(0, 3 * SHARD), pl.ds(0, HALF)], s_w.at[2])
     wait_bytes(rbuf.at[pl.ds(0, 3)], s_res.at[0])
     wait_bytes(mbuf.at[pl.ds(0, 3)], s_res.at[1])
     wait_bytes(att.at[pl.ds(0, 3)], s_g.at[0])
-    wait_bytes(gbuf.at[:, :, pl.ds(0, 1024)], s_y.at[0])
-    wait_bytes(gbuf.at[:, :, pl.ds(0, 512)], s_y.at[1])
+    wait_bytes(gbuf.at[:, :, pl.ds(0, 3 * 512)], s_y.at[0])
     wait_bytes(msg.at[pl.ds(0, 3)], s_msg.at[0])
     for finish in finishes:
         finish()
@@ -622,12 +617,12 @@
             pltpu.VMEM((BAND + 2 * WIN, HD), BF16),
             pltpu.VMEM((BAND + 2 * WIN, HD), BF16),
             pltpu.VMEM((4, 4, BLOCK, HD), BF16),
-            pltpu.VMEM((4, DEEP, SHARD), BF16),
-            pltpu.VMEM((DEEP, QUARTER), BF16),
+            pltpu.VMEM((QUARTER, PAD_DEEP), BF16),
+            pltpu.VMEM((128, QUARTER), BF16),
             pltpu.VMEM((4, BLOCK, QUARTER), BF16),
             pltpu.VMEM((4, BLOCK, RANKS), BF16),
             pltpu.VMEM((4, BLOCK, DEEP), BF16),
-            pltpu.VMEM((512, QUARTER), F32),
+            pltpu.VMEM((BLOCK, QUARTER), F32),
             pltpu.VMEM((4, BLOCK + 8, 128), F32),
             pltpu.VMEM((4, BLOCK + 8, 128), F32),
             pltpu.VMEM((BLOCK, 128), BF16),
@@ -647,17 +642,15 @@
             dma((2,)),
             dma((4,)),
             dma((1,)),
-            dma((4, 4)),
-            dma((2,)),
+            dma((4,)),
             dma((1,)),
             dma((1,)),
             dma((1,)),
-            dma((9,)),
-            dma((2,)),
-            dma((2,)),
+            dma((3,)),
+            dma((27,)),
         ],
         compiler_params=pltpu.CompilerParams(
-            collective_id=0, has_side_effects=True, vmem_limit_bytes=48 * 1024 * 1024
+            collective_id=0, has_side_effects=True, vmem_limit_bytes=60 * 1024 * 1024
         ),
     )(
         queries,
@@ -667,12 +660,12 @@
         request_adapter,
         residual,
         output_gate.reshape(1, -1),
-        output_weight,
+        output_weight.T,
         adapter_down_factors,
-        adapter_up_factors,
+        adapter_up_factors.T,
         closing_scale.reshape(1, -1),
         closing_shift.reshape(1, -1),
-        patch_projection_weight,
+        patch_projection_weight.T,
         patch_projection_bias.reshape(1, -1),
         convolution_kernel,
         convolution_bias.reshape(1, -1),

time: 131 us -> 115 us (0.88)
  Pallas kernels: 122 us -> 111 us
  local copies, waits for them, and re-layouts: 7.77 us -> 1.88 us
    pallas_call x1, Pallas kernels: 122 us -> 111 us  [on_device(): pl.pallas_call(kernel, out_shape=jax.ShapeDtypeStruct((16, 32, 512), BF16...]
    unnamed x30 -> x1, local copies, waits for them, and re-layouts: 7.77 us -> 1.88 us
where the time goes in v2:
time: 115 us; the launch traced here: 113 us
  Pallas kernels  111 us (97%)
  local copies, waits for them, and re-layouts  1.88 us (2%)
    pallas_call x1, Pallas kernels, on_device(): pl.pallas_call(kernel, out_shape=jax.ShapeDtypeStruct((16, 32, 512), BF16...  111 us

profile of v2, /device:TPU:1, one launch (start us, length us, event | category | flops | bytes accessed | tf_op | source)
XLA Modules:
  0.0 113.3 jit_solution(2831319403536216482)
XLA Ops:
  0.0 111.4 %shard_map.154 = bf16[16,32,512]{2,1,0:T(8,128)(2,1)} custom-call(bf16[128,2048]{1,0:T(8,128)(2,1)} %q_hbm.1, bf16[128,2048]{1,0:T(8,128)(2,1)} %k_hbm.1, bf16[128,2048]{1,0:T(8,128)(2,1)} %v_hbm.1, s32[1,128]{1,0:T(1,128)} %bitcast.16, s32[8]{0:T(128)} %request_adapter.1, bf16[128,3072]{1,0:T(8,128)(2,1)} %residual_hbm.1, f32[1,3072]{1,0:T(1,128)} %bitcast.12, ...), custom_call_target="tpu_custom_call" | custom-call | tf_op jit(solution)/shard_map/pallas_call | solution.py:607
  111.4 1.9 %copy.18 = bf16[16,32,512]{2,1,0:T(8,128)(2,1)} copy(bf16[16,32,512]{2,1,0:T(8,128)(2,1)} %shard_map.154) | data formatting | bytes 1048576

commit v3 on v2

--- a/solution.py
+++ b/solution.py
@@ -195,15 +195,16 @@
     def piece(z2):
         return wq.at[pl.ds(pl.multiple_of(z2 * SHARD + x * PIECE, 16), PIECE), half_cols]
 
-    w_local.wait()
-    u_local.wait()
-    for d in (1, -1, two):
-        remote(piece(z), piece(z), s_w.at[0], r_w.at[0], ring(d)).start()
 
     own_rows = pl.ds(pl.multiple_of(WIN + t * BLOCK, BLOCK), BLOCK)
     own_q_rows = pl.ds(pl.multiple_of(t * BLOCK, BLOCK), BLOCK)
     sets = ((k_hbm, kbuf, own_rows), (v_hbm, vbuf, own_rows), (q_hbm, qbuf, own_q_rows))
     for a, (src, dst, rows) in enumerate(sets):
+        if a == 2:
+            w_local.wait()
+            u_local.wait()
+            for d in (1, -1, two):
+                remote(piece(z), piece(z), s_w.at[0], r_w.at[0], ring(d)).start()
 
         def send(d, carry, a=a, src=src, dst=dst, rows=rows):
             p = lax.rem(t + d, TILE)
@@ -284,12 +285,6 @@
         preferred_element_type=F32,
     )
 
-    wait_bytes(wq.at[pl.ds(0, 9 * PIECE), pl.ds(0, HALF)], r_w.at[1])
-    for d in range(1, 4):
-        z2 = lax.rem(z + d, 4)
-        ref = wq.at[pl.ds(pl.multiple_of(z2 * SHARD, 64), SHARD), half_cols]
-        remote(ref, ref, s_w.at[2], r_w.at[2], {"seq": sibling}).start()
-
     for row in (3, 0):
         for a in range(2):
             buf = (kbuf, vbuf)[a]
@@ -304,15 +299,20 @@
         dst = buf.at[pl.ds(WIN + BAND, WIN), :]
         return remote(src, dst, s_halo.at[1], r_halo.at[1], {"seq": s - 1})
 
-    @pl.when(jnp.logical_not(last))
-    def _():
-        halo(kbuf, 0, True).start()
-        halo(vbuf, 1, True).start()
-
-    @pl.when(jnp.logical_not(first))
-    def _():
-        halo(kbuf, 0, False).start()
-        halo(vbuf, 1, False).start()
+    def send_halo(row):
+        @pl.when((row == 3) & jnp.logical_not(last))
+        def _():
+            halo(kbuf, 0, True).start()
+            halo(vbuf, 1, True).start()
+
+        @pl.when((row == 0) & jnp.logical_not(first))
+        def _():
+            halo(kbuf, 0, False).start()
+            halo(vbuf, 1, False).start()
+
+    row_a = jnp.where(core == 0, 3, 0)
+    row_b = 3 - row_a
+    send_halo(row_a)
 
     for row in (1, 2):
         for a in range(2):
@@ -324,6 +324,41 @@
     factor = math.log2(math.e) / math.sqrt(HD)
     row_at = lax.broadcasted_iota(jnp.int32, (BLOCK, BLOCK), 0)
     col_at = lax.broadcasted_iota(jnp.int32, (BLOCK, BLOCK), 1)
+
+    head_cols = pl.ds(pl.multiple_of(t * HD, HD), HD)
+
+    def send_heads(row, b):
+        @pl.when(z == b)
+        def _():
+            dst = gbuf.at[row, :, head_cols]
+            pltpu.make_async_copy(att.at[row, b], dst, r_g.at[row, z]).start()
+            for d in range(1, 4):
+                where = {"tile": lax.rem(y + d, 4) * 4 + z}
+                remote(att.at[row, b], dst, s_y.at[0], r_y.at[row], where).start()
+
+        @pl.when(z != b)
+        def _():
+            remote(
+                att.at[row, b],
+                gbuf.at[row, :, head_cols],
+                s_g.at[0],
+                r_g.at[row, z],
+                {"tile": y * 4 + b},
+            ).start()
+
+    def send_group(row):
+        order = (
+            jnp.where(z < 3, z + 1, 2),
+            jnp.where(z == 0, 2, jnp.where(z == 3, 1, z - 1)),
+            jnp.where(z < 2, 3, 0),
+        )
+        for z2 in order:
+            ref = gbuf.at[row, :, pl.ds(pl.multiple_of((y * 4 + z2) * HD, HD), HD)]
+            wait_bytes(gbuf.at[row, :, pl.ds(0, HD)], r_g.at[row, z2])
+            for d in range(1, 4):
+                where = {"tile": lax.rem(y + d, 4) * 4 + z}
+                remote(ref, ref, s_y.at[0], r_y.at[row], where).start()
+        wait_bytes(gbuf.at[row, :, pl.ds(0, HD)], r_g.at[row, z])
 
     def attend(row):
         edge = (first & (row == 0)) | (last & (row == 3))
@@ -349,6 +384,7 @@
             totals = jnp.sum(expons, axis=1, keepdims=True)
             weighted = jnp.dot(expons.astype(BF16), v, preferred_element_type=F32)
             att[row, b] = (weighted / totals).astype(BF16)
+            send_heads(row, b)
 
         @pl.when(edge)
         def _():
@@ -359,32 +395,6 @@
         def _():
             for b in range(4):
                 block(b, False)
-
-    head_cols = pl.ds(pl.multiple_of(t * HD, HD), HD)
-
-    def send_heads(row):
-        pltpu.make_async_copy(
-            att.at[row, z], gbuf.at[row, :, head_cols], r_g.at[row]
-        ).start()
-        for d in range(1, 4):
-            z2 = lax.rem(z + d, 4)
-            remote(
-                att.at[row, z2],
-                gbuf.at[row, :, head_cols],
-                s_g.at[0],
-                r_g.at[row],
-                {"tile": y * 4 + z2},
-            ).start()
-
-    def send_group(row):
-        wait_bytes(gbuf.at[row, :, pl.ds(0, 512)], r_g.at[row])
-        ref = gbuf.at[row, :, pl.ds(pl.multiple_of(y * 512, 128), 512)]
-        for d in range(1, 4):
-            where = {"tile": lax.rem(y + d, 4) * 4 + z}
-            remote(ref, ref, s_y.at[0], r_y.at[row], where).start()
-
-    row_a = jnp.where(core == 0, 3, 0)
-    row_b = 3 - row_a
 
     def wait_halo(row):
         missing = (first & (row == 0)) | (last & (row == 3))
@@ -432,14 +442,85 @@
             where = {"tile": row * 4 + z}
             remote(msg.at[row], msgin.at[y], s_msg.at[0], r_msg.at[0], where).start()
 
+    half = lax.rem(t, 2)
+    line = t // 2 + 1
+
+    def hand(i, target, src, dst, shift, sending):
+        recv = r_lat.at[y if shift == 0 else 4 if shift == 1 else 5]
+        if shift == 0:
+            far = remote(src, dst, s_lat.at[i], recv, {"tile": target})
+            away = target != t
+        else:
+            where = {"seq": s + shift, "tile": target}
+            far = remote(src, dst, s_lat.at[i], recv, where)
+            away = sending
+
+        def begin():
+            if shift == 0:
+
+                @pl.when(target == t)
+                def _():
+                    pltpu.make_async_copy(src, dst, recv).start()
+
+            @pl.when(away)
+            def _():
+                far.start()
+
+        def finish():
+            @pl.when(away)
+            def _():
+                far.wait_send()
+
+        return begin, finish
+
+    hands = []
+    cross_src = pl.ds(pl.multiple_of(112 * (1 - half), 16), 16)
+    cross_dst = pl.ds(pl.multiple_of(32 * half, 16), 16)
+    for k, (shift, sending, at) in enumerate(((1, bottom, 0), (-1, top, 9), (0, None, line))):
+        for i in range(8):
+            begin = max(0, i - 1) * 16
+            size = min(8, i + 2) * 16 - begin
+            src = lat.at[pl.ds(begin, size), :]
+            dst = lbuf.at[at, pl.ds(16 if i == 0 else 0, size), :]
+            hands.append(hand(9 * k + i, half * 8 + i, src, dst, shift, sending))
+        src = lat.at[cross_src, :]
+        dst = lbuf.at[at, cross_dst, :]
+        hands.append(hand(9 * k + 8, 8 - half, src, dst, shift, sending))
+    def finish_home():
+        wait_bytes(msgin, r_msg.at[0])
+
+        means = [msgin[i, 0:BLOCK, 64:65] for i in range(4)]
+        spreads = [msgin[i, 0:BLOCK, 65:66] for i in range(4)]
+        overall = (means[0] + means[1] + means[2] + means[3]) * 0.25
+        variance = spreads[0] + spreads[1] + spreads[2] + spreads[3]
+        projected = jnp.zeros((BLOCK, 128), F32)
+        constant = bias_row[0:1, :]
+        for i in range(4):
+            off = means[i] - overall
+            variance = variance + QUARTER * off * off
+            projected = projected + (
+                msgin[i, 0:BLOCK, :] + off * msgin[i, BLOCK : BLOCK + 1, :]
+            )
+            constant = constant + msgin[i, BLOCK + 1 : BLOCK + 2, :]
+        projected = projected * lax.rsqrt(variance * (1.0 / WIDTH) + norm_epsilon) + constant
+        latents = projected / latent_scaling + latent_offset
+        small = lax.broadcasted_iota(jnp.int32, (BLOCK, 128), 1) < 64
+        lat[...] = jnp.where(small, latents, 0.0).astype(BF16)
+
+        for begin, _ in hands:
+            begin()
+
     attend(1)
-    send_heads(1)
     attend(2)
-    send_heads(2)
-    send_group(1)
     wait_halo(row_a)
     attend(row_a)
-    send_heads(row_a)
+    send_halo(row_b)
+    wait_bytes(wq.at[pl.ds(0, 9 * PIECE), pl.ds(0, HALF)], r_w.at[1])
+    for d in range(1, 4):
+        z2 = lax.rem(z + d, 4)
+        ref = wq.at[pl.ds(pl.multiple_of(z2 * SHARD, 64), SHARD), half_cols]
+        remote(ref, ref, s_w.at[2], r_w.at[2], {"seq": sibling}).start()
+    send_group(1)
     send_group(2)
     wait_bytes(wq.at[pl.ds(0, 3 * SHARD), pl.ds(0, HALF)], r_w.at[2])
     wait_bytes(rbuf, r_res.at[0])
@@ -448,73 +529,20 @@
     send_group(row_a)
     wait_halo(row_b)
     attend(row_b)
-    send_heads(row_b)
     project(2)
     send_group(row_b)
     project(row_a)
+
+    @pl.when(y != row_b)
+    def _():
+        finish_home()
+
     project(row_b)
-    wait_bytes(msgin, r_msg.at[0])
-
-    means = [msgin[i, 0:BLOCK, 64:65] for i in range(4)]
-    spreads = [msgin[i, 0:BLOCK, 65:66] for i in range(4)]
-    overall = (means[0] + means[1] + means[2] + means[3]) * 0.25
-    variance = spreads[0] + spreads[1] + spreads[2] + spreads[3]
-    projected = jnp.zeros((BLOCK, 128), F32)
-    constant = bias_row[0:1, :]
-    for i in range(4):
-        off = means[i] - overall
-        variance = variance + QUARTER * off * off
-        projected = projected + (
-            msgin[i, 0:BLOCK, :] + off * msgin[i, BLOCK : BLOCK + 1, :]
-        )
-        constant = constant + msgin[i, BLOCK + 1 : BLOCK + 2, :]
-    projected = projected * lax.rsqrt(variance * (1.0 / WIDTH) + norm_epsilon) + constant
-    latents = projected / latent_scaling + latent_offset
-    small = lax.broadcasted_iota(jnp.int32, (BLOCK, 128), 1) < 64
-    lat[...] = jnp.where(small, latents, 0.0).astype(BF16)
-
-    half = lax.rem(t, 2)
-    line = t // 2 + 1
-
-    def hand(i, target, src, dst, shift, sending):
-        recv = r_lat.at[shift % 3]
-        if shift == 0:
-            far = remote(src, dst, s_lat.at[i], recv, {"tile": target})
-            near = pltpu.make_async_copy(src, dst, recv)
-            away = target != t
-
-            @pl.when(target == t)
-            def _():
-                near.start()
-        else:
-            where = {"seq": s + shift, "tile": target}
-            far = remote(src, dst, s_lat.at[i], recv, where)
-            away = sending
-
-        @pl.when(away)
-        def _():
-            far.start()
-
-        def finish():
-            @pl.when(away)
-            def _():
-                far.wait_send()
-
-        return finish
-
-    finishes = []
-    cross_src = pl.ds(pl.multiple_of(112 * (1 - half), 16), 16)
-    cross_dst = pl.ds(pl.multiple_of(32 * half, 16), 16)
-    for k, (shift, sending, at) in enumerate(((1, bottom, 0), (-1, top, 9), (0, None, line))):
-        for i in range(8):
-            begin = max(0, i - 1) * 16
-            size = min(8, i + 2) * 16 - begin
-            src = lat.at[pl.ds(begin, size), :]
-            dst = lbuf.at[at, pl.ds(16 if i == 0 else 0, size), :]
-            finishes.append(hand(9 * k + i, half * 8 + i, src, dst, shift, sending))
-        src = lat.at[cross_src, :]
-        dst = lbuf.at[at, cross_dst, :]
-        finishes.append(hand(9 * k + 8, 8 - half, src, dst, shift, sending))
+
+    @pl.when(y == row_b)
+    def _():
+        finish_home()
+
     side = (t == 0) | (t == TILE - 1)
 
     def wait_lines(begin, count, sem):
@@ -526,38 +554,55 @@
         def _():
             wait_bytes(lbuf.at[pl.ds(begin, count), :, :], sem)
 
-    wait_lines(1, 8, r_lat.at[0])
-
-    @pl.when(jnp.logical_not(first))
-    def _():
-        wait_lines(0, 1, r_lat.at[1])
-
-    @pl.when(jnp.logical_not(last))
-    def _():
-        wait_lines(9, 1, r_lat.at[2])
-
-    lfull[...] = lbuf[...].astype(F32)
-    columns = [lfull[:, 15 + i : 31 + i, :].astype(BF16) for i in range(3)]
-    for a in range(2):
-        for b in range(2):
-            near = jnp.concatenate(
-                [
-                    columns[j + b][i + a : i + a + 8].reshape(128, 128)
-                    for i in range(2)
-                    for j in range(2)
-                ],
-                axis=1,
-            )
-            value = (
-                jnp.dot(near, wc[2 * a + b], preferred_element_type=F32) + conv_bias[...]
-            ).reshape(8, 16, 512)
-            for r in range(8):
-                for c in range(4):
-                    obuf[c, 2 * r + a, pl.ds(b, 16, stride=2), :] = value[
-                        r, :, c * 128 : (c + 1) * 128
-                    ]
-    for c in range(4):
-        out[:, :, c * 128 : (c + 1) * 128] = obuf[c].astype(BF16)
+    def convolve(begin, count):
+        lines = pl.ds(begin, count + 2)
+        lfull[lines] = lbuf[lines].astype(F32)
+        columns = [lfull[lines, 15 + i : 31 + i, :].astype(BF16) for i in range(3)]
+        for a in range(2):
+            for b in range(2):
+                near = jnp.concatenate(
+                    [
+                        columns[j + b][i + a : i + a + count].reshape(16 * count, 128)
+                        for i in range(2)
+                        for j in range(2)
+                    ],
+                    axis=1,
+                )
+                value = (
+                    jnp.dot(near, wc[2 * a + b], preferred_element_type=F32) + conv_bias[...]
+                ).reshape(count, 16, 512)
+                for r in range(count):
+                    for c in range(4):
+                        obuf[c, 2 * (begin + r) + a, pl.ds(b, 16, stride=2), :] = value[
+                            r, :, c * 128 : (c + 1) * 128
+                        ]
+        rows = pl.ds(2 * begin, 2 * count)
+        for c in range(4):
+            out[rows, :, c * 128 : (c + 1) * 128] = obuf[c, rows].astype(BF16)
+
+    for row in (1, 2, row_a):
+        wait_lines(2 * row + 1, 2, r_lat.at[row])
+
+    @pl.when((core == 0) & jnp.logical_not(last))
+    def _():
+        wait_lines(9, 1, r_lat.at[5])
+
+    @pl.when((core == 1) & jnp.logical_not(first))
+    def _():
+        wait_lines(0, 1, r_lat.at[4])
+
+    convolve(jnp.where(core == 0, 3, 0), 5)
+    wait_lines(2 * row_b + 1, 2, r_lat.at[row_b])
+
+    @pl.when((core == 0) & jnp.logical_not(first))
+    def _():
+        wait_lines(0, 1, r_lat.at[4])
+
+    @pl.when((core == 1) & jnp.logical_not(last))
+    def _():
+        wait_lines(9, 1, r_lat.at[5])
+
+    convolve(jnp.where(core == 0, 0, 5), 3)
 
     for a in range(3):
         wait_bytes(kbuf.at[pl.ds(0, 15 * BLOCK), :], s_qkv.at[a])
@@ -578,7 +623,7 @@
     wait_bytes(att.at[pl.ds(0, 3)], s_g.at[0])
     wait_bytes(gbuf.at[:, :, pl.ds(0, 3 * 512)], s_y.at[0])
     wait_bytes(msg.at[pl.ds(0, 3)], s_msg.at[0])
-    for finish in finishes:
+    for _, finish in hands:
         finish()
 
 
@@ -640,13 +685,13 @@
             dma((3,)),
             dma((2,)),
             dma((2,)),
-            dma((4,)),
+            dma((4, 4)),
             dma((1,)),
             dma((4,)),
             dma((1,)),
             dma((1,)),
             dma((1,)),
-            dma((3,)),
+            dma((6,)),
             dma((27,)),
         ],
         compiler_params=pltpu.CompilerParams(

time: 115 us -> 109 us (0.948)
  the two profiles are of different devices: /device:TPU:1 before, /device:TPU:28 now
where the time goes in v3:
time: 109 us
  Pallas kernels  107 us (98%)
  local copies, waits for them, and re-layouts  1.88 us (2%)
    pallas_call x1, Pallas kernels, on_device(): pl.pallas_call(kernel, out_shape=jax.ShapeDtypeStruct((16, 32, 512), BF16...  107 us

profile of v3, /device:TPU:28, one launch (start us, length us, event | category | flops | bytes accessed | tf_op | source)
XLA Modules:
  0.0 108.7 jit_solution(723360304413294107)
XLA Ops:
  0.0 106.8 %shard_map.154 = bf16[16,32,512]{2,1,0:T(8,128)(2,1)} custom-call(bf16[128,2048]{1,0:T(8,128)(2,1)} %q_hbm.1, bf16[128,2048]{1,0:T(8,128)(2,1)} %k_hbm.1, bf16[128,2048]{1,0:T(8,128)(2,1)} %v_hbm.1, s32[1,128]{1,0:T(1,128)} %bitcast.16, s32[8]{0:T(128)} %request_adapter.1, bf16[128,3072]{1,0:T(8,128)(2,1)} %residual_hbm.1, f32[1,3072]{1,0:T(1,128)} %bitcast.12, ...), custom_call_target="tpu_custom_call" | custom-call | tf_op jit(solution)/shard_map/pallas_call | solution.py:652
  106.9 1.9 %copy.18 = bf16[16,32,512]{2,1,0:T(8,128)(2,1)} copy(bf16[16,32,512]{2,1,0:T(8,128)(2,1)} %shard_map.154) | data formatting | bytes 1048576

commit v4 on v3

--- a/solution.py
+++ b/solution.py
@@ -200,11 +200,6 @@
     own_q_rows = pl.ds(pl.multiple_of(t * BLOCK, BLOCK), BLOCK)
     sets = ((k_hbm, kbuf, own_rows), (v_hbm, vbuf, own_rows), (q_hbm, qbuf, own_q_rows))
     for a, (src, dst, rows) in enumerate(sets):
-        if a == 2:
-            w_local.wait()
-            u_local.wait()
-            for d in (1, -1, two):
-                remote(piece(z), piece(z), s_w.at[0], r_w.at[0], ring(d)).start()
 
         def send(d, carry, a=a, src=src, dst=dst, rows=rows):
             p = lax.rem(t + d, TILE)
@@ -237,13 +232,10 @@
             ).start()
             remote(mbuf.at[y], mbuf.at[y], s_res.at[1], r_res.at[1], where).start()
 
-    wait_bytes(wq.at[pl.ds(0, 3 * PIECE), pl.ds(0, HALF)], r_w.at[0])
-    for d in range(1, 4):
-        ref = piece(lax.rem(z + d, 4))
-        for e in range(1, 4):
-            remote(
-                ref, ref, s_w.at[1], r_w.at[1], {"seq": lax.rem(s + 8 * e, SEQ)}
-            ).start()
+    w_local.wait()
+    u_local.wait()
+    for d in (1, -1, two):
+        remote(piece(z), piece(z), s_w.at[0], r_w.at[0], ring(d)).start()
 
     flat_kernel = conv_kernel[...].reshape(144, 512)
     place = lax.broadcasted_iota(jnp.int32, (512, 144), 0)
@@ -429,9 +421,10 @@
             (centered * gain).astype(BF16), patch_wide[...], across, preferred_element_type=F32
         )
         lane_at = lax.broadcasted_iota(jnp.int32, (BLOCK, 128), 1)
-        part = jnp.where(lane_at == 64, average, jnp.where(lane_at == 65, squares, part))
-        msg[row, 0:BLOCK, :] = part
-        msg[row, BLOCK : BLOCK + 8, :] = sums
+        stats = jnp.where(lane_at == 0, average, jnp.where(lane_at == 1, squares, 0.0))
+        msg[row, 0:64, :] = part[0:64] + pltpu.roll(part[64:BLOCK], 64, axis=1)
+        msg[row, 64:72, :] = stats.T[0:8]
+        msg[row, 72:80, :] = sums
 
         @pl.when(row == y)
         def _():
@@ -489,19 +482,21 @@
     def finish_home():
         wait_bytes(msgin, r_msg.at[0])
 
-        means = [msgin[i, 0:BLOCK, 64:65] for i in range(4)]
-        spreads = [msgin[i, 0:BLOCK, 65:66] for i in range(4)]
+        packed = msgin[0, 0:64, :] + msgin[1, 0:64, :] + msgin[2, 0:64, :] + msgin[3, 0:64, :]
+        projected = jnp.concatenate([packed, pltpu.roll(packed, 64, axis=1)], axis=0)
+        stats = jnp.concatenate(
+            [msgin[i, 64:72, :] for i in range(4)] + [jnp.zeros((96, 128), F32)], axis=0
+        ).T
+        means = [stats[:, 8 * i : 8 * i + 1] for i in range(4)]
+        spreads = [stats[:, 8 * i + 1 : 8 * i + 2] for i in range(4)]
         overall = (means[0] + means[1] + means[2] + means[3]) * 0.25
         variance = spreads[0] + spreads[1] + spreads[2] + spreads[3]
-        projected = jnp.zeros((BLOCK, 128), F32)
         constant = bias_row[0:1, :]
         for i in range(4):
             off = means[i] - overall
             variance = variance + QUARTER * off * off
-            projected = projected + (
-                msgin[i, 0:BLOCK, :] + off * msgin[i, BLOCK : BLOCK + 1, :]
-            )
-            constant = constant + msgin[i, BLOCK + 1 : BLOCK + 2, :]
+            projected = projected + off * msgin[i, 72:73, :]
+            constant = constant + msgin[i, 73:74, :]
         projected = projected * lax.rsqrt(variance * (1.0 / WIDTH) + norm_epsilon) + constant
         latents = projected / latent_scaling + latent_offset
         small = lax.broadcasted_iota(jnp.int32, (BLOCK, 128), 1) < 64
@@ -512,34 +507,43 @@
 
     attend(1)
     attend(2)
+    wait_bytes(wq.at[pl.ds(0, 3 * PIECE), pl.ds(0, HALF)], r_w.at[0])
+    for d in range(1, 4):
+        ref = piece(lax.rem(z + d, 4))
+        for e in range(1, 4):
+            remote(
+                ref, ref, s_w.at[1], r_w.at[1], {"seq": lax.rem(s + 8 * e, SEQ)}
+            ).start()
     wait_halo(row_a)
     attend(row_a)
     send_halo(row_b)
+    send_group(1)
+    send_group(2)
+    send_group(row_a)
     wait_bytes(wq.at[pl.ds(0, 9 * PIECE), pl.ds(0, HALF)], r_w.at[1])
     for d in range(1, 4):
         z2 = lax.rem(z + d, 4)
         ref = wq.at[pl.ds(pl.multiple_of(z2 * SHARD, 64), SHARD), half_cols]
         remote(ref, ref, s_w.at[2], r_w.at[2], {"seq": sibling}).start()
-    send_group(1)
-    send_group(2)
+    wait_halo(row_b)
+    attend(row_b)
     wait_bytes(wq.at[pl.ds(0, 3 * SHARD), pl.ds(0, HALF)], r_w.at[2])
     wait_bytes(rbuf, r_res.at[0])
     wait_bytes(mbuf.at[pl.ds(0, 3)], r_res.at[1])
     project(1)
-    send_group(row_a)
-    wait_halo(row_b)
-    attend(row_b)
+    send_group(row_b)
     project(2)
-    send_group(row_b)
     project(row_a)
 
-    @pl.when(y != row_b)
+    inner = (y == 1) | (y == 2)
+
+    @pl.when(inner)
     def _():
         finish_home()
 
     project(row_b)
 
-    @pl.when(y == row_b)
+    @pl.when(jnp.logical_not(inner))
     def _():
         finish_home()
 
@@ -668,8 +672,8 @@
             pltpu.VMEM((4, BLOCK, RANKS), BF16),
             pltpu.VMEM((4, BLOCK, DEEP), BF16),
             pltpu.VMEM((BLOCK, QUARTER), F32),
-            pltpu.VMEM((4, BLOCK + 8, 128), F32),
-            pltpu.VMEM((4, BLOCK + 8, 128), F32),
+            pltpu.VMEM((4, 80, 128), F32),
+            pltpu.VMEM((4, 80, 128), F32),
             pltpu.VMEM((BLOCK, 128), BF16),
             pltpu.VMEM((10, 48, 128), BF16),
             pltpu.VMEM((10, 48, 128), F32),

time: 109 us -> 105 us (0.963)
  the two profiles are of different devices: /device:TPU:28 before, /device:TPU:1 now
where the time goes in v4:
time: 105 us; the launch traced here: 104 us
  Pallas kernels  102 us (97%)
  local copies, waits for them, and re-layouts  1.88 us (2%)
    pallas_call x1, Pallas kernels, on_device(): pl.pallas_call(kernel, out_shape=jax.ShapeDtypeStruct((16, 32, 512), BF16...  102 us

profile of v4, /device:TPU:1, one launch (start us, length us, event | category | flops | bytes accessed | tf_op | source)
XLA Modules:
  0.0 104.3 jit_solution(15081518114056553542)
XLA Ops:
  0.0 102.5 %shard_map.154 = bf16[16,32,512]{2,1,0:T(8,128)(2,1)} custom-call(bf16[128,2048]{1,0:T(8,128)(2,1)} %q_hbm.1, bf16[128,2048]{1,0:T(8,128)(2,1)} %k_hbm.1, bf16[128,2048]{1,0:T(8,128)(2,1)} %v_hbm.1, s32[1,128]{1,0:T(1,128)} %bitcast.16, s32[8]{0:T(128)} %request_adapter.1, bf16[128,3072]{1,0:T(8,128)(2,1)} %residual_hbm.1, f32[1,3072]{1,0:T(1,128)} %bitcast.12, ...), custom_call_target="tpu_custom_call" | custom-call | tf_op jit(solution)/shard_map/pallas_call | solution.py:656
  102.5 1.9 %copy.18 = bf16[16,32,512]{2,1,0:T(8,128)(2,1)} copy(bf16[16,32,512]{2,1,0:T(8,128)(2,1)} %shard_map.154) | data formatting | bytes 1048576

commit v5 on v4

--- a/solution.py
+++ b/solution.py
@@ -213,6 +213,11 @@
         own_cols = pl.ds(pl.multiple_of(t * HD, HD), HD)
         pltpu.make_async_copy(src.at[:, own_cols], dst.at[rows, :], r_qkv.at[a, y]).start()
 
+    w_local.wait()
+    u_local.wait()
+    for d in (1, -1, two):
+        remote(piece(z), piece(z), s_w.at[0], r_w.at[0], ring(d)).start()
+
     adapters = jnp.zeros((1, BLOCK), jnp.int32)
     for r in range(8):
         adapters = adapters + jnp.where(request[...] == r, request_adapter[r], 0)
@@ -232,10 +237,6 @@
             ).start()
             remote(mbuf.at[y], mbuf.at[y], s_res.at[1], r_res.at[1], where).start()
 
-    w_local.wait()
-    u_local.wait()
-    for d in (1, -1, two):
-        remote(piece(z), piece(z), s_w.at[0], r_w.at[0], ring(d)).start()
 
     flat_kernel = conv_kernel[...].reshape(144, 512)
     place = lax.broadcasted_iota(jnp.int32, (512, 144), 0)

time: 105 us -> 105 us (level)
  no operation moved by 1% of the time
where the time goes in v5:
time: 105 us; the launch traced here: 104 us
  Pallas kernels  102 us (97%)
  local copies, waits for them, and re-layouts  1.88 us (2%)
    pallas_call x1, Pallas kernels, on_device(): pl.pallas_call(kernel, out_shape=jax.ShapeDtypeStruct((16, 32, 512), BF16...  102 us

profile of v5, /device:TPU:1, one launch (start us, length us, event | category | flops | bytes accessed | tf_op | source)
XLA Modules:
  0.0 104.4 jit_solution(10999803050634297866)
XLA Ops:
  0.0 102.5 %shard_map.154 = bf16[16,32,512]{2,1,0:T(8,128)(2,1)} custom-call(bf16[128,2048]{1,0:T(8,128)(2,1)} %q_hbm.1, bf16[128,2048]{1,0:T(8,128)(2,1)} %k_hbm.1, bf16[128,2048]{1,0:T(8,128)(2,1)} %v_hbm.1, s32[1,128]{1,0:T(1,128)} %bitcast.16, s32[8]{0:T(128)} %request_adapter.1, bf16[128,3072]{1,0:T(8,128)(2,1)} %residual_hbm.1, f32[1,3072]{1,0:T(1,128)} %bitcast.12, ...), custom_call_target="tpu_custom_call" | custom-call | tf_op jit(solution)/shard_map/pallas_call | solution.py:657
  102.5 1.9 %copy.18 = bf16[16,32,512]{2,1,0:T(8,128)(2,1)} copy(bf16[16,32,512]{2,1,0:T(8,128)(2,1)} %shard_map.154) | data formatting | bytes 1048576
